TPU v7x, 32 devices: a whole 2x2x4 slice. The times are simulated.
32 devices in a mesh: groups: 2 (over x), tensor: 8 (over z, y), pool: 2 (over core).
Axes of the slice: x: 2, y: 2, z: 4, core: 2. Of those that a mesh axis runs over, the one named last changes fastest.
Arguments:
- inputs: bfloat16 [2, 256, 8192], P(None, ('groups', 'pool')), parts along dimension 1, may hold values from -6 to 6
- query_weight: bfloat16 [8192, 8192], P(None, 'tensor'), may hold values from -0.0625 to 0.0625
- key_value_weight: bfloat16 [8192, 1024], P(None, 'tensor'), may hold values from -0.0625 to 0.0625
- key_value_cache: bfloat16 [256, 8, 2, 128, 128], P(('groups', 'pool'), 'tensor'), parts along dimension 0, may hold values from -330 to 330
- lengths: int32 [256], P(('groups', 'pool')), parts along dimension 0, may hold values from 1 to 256, as said below
- request_adapter: int32 [256], P(('groups', 'pool')), parts along dimension 0, may hold values from 0 to 255, as said below
- adapter_storage_row: int32 [512], P('groups'), parts along dimension 0, may hold values from 0 to 255, as said below
- adapter_down_factors: bfloat16 [512, 64, 8192], P(('groups', 'tensor', 'pool')), parts along dimension 0, may hold values from -0.0625 to 0.0625
- adapter_up_factors: bfloat16 [512, 64, 8192], P(('groups', 'tensor', 'pool')), parts along dimension 0, may hold values from -0.75 to 0.75
Outputs:
- attended: bfloat16 [2, 256, 8192], P(None, ('groups', 'pool'), 'tensor'), parts along dimension 1
There are 2 independent parts, one for each index of `groups`. A program takes and returns all parts, laid end to end along the dimension named above; an argument that names none is the same for every part. Nothing has to cross between parts.
Inputs may be any that keep to these rules, and one draw needn't show every extreme that they name: `adapter_storage_row`: storage row r lies on device r // 16 of tensor and pool taken together, tensor index major; every row appears once. `request_adapter`: among the 64 requests of one pool index, at most 8 use adapters stored on the same device; in every group one device holds the adapters of exactly 8 requests of every pool index. `lengths`: every pool index has a request of length 256.
All inputs are finite; a program needn't handle non-finite values.
Results may differ from a plain program's by a relative error of at most 0.012.
Values may be sent and summed in bfloat16 or wider, within the bound.
No kernel may reach another device: no remote copies, remote signals or barrier semaphores. Data moves between devices by JAX's collectives and lax.ppermute only.
A program may use at most 320 MiB of HBM per device.

v0:
```python
import jax
import jax.numpy as jnp
from jax import lax
from jax.sharding import PartitionSpec as P

ROPE_BASE = 500000.0
ADAPTER_SCALE = 0.5
MASKED = -1e30


def swapped(value, axis, bit):
    mask = 2**bit
    pairs = [(source, source ^ mask) for source in range(lax.axis_size(axis))]
    return lax.ppermute(value, axis, pairs)


def rotate(vector, position):
    half = vector.shape[-1] // 2
    freq = ROPE_BASE ** (-2.0 * jnp.arange(half, dtype=jnp.float32) / vector.shape[-1])
    angle = position.astype(jnp.float32)[..., None] * freq
    cosine = jnp.cos(angle)
    sine = jnp.sin(angle)
    first = vector[..., :half]
    second = vector[..., half:]
    return jnp.concatenate(
        [first * cosine - second * sine, second * cosine + first * sine], axis=-1
    )


def score_block(query_group, cached_keys, new_keys, lengths):
    scale = query_group.shape[-1] ** (-0.5)
    cached = (
        jnp.einsum("srgd,rjd->srgj", query_group, cached_keys, preferred_element_type=jnp.float32)
        * scale
    )
    valid = jnp.arange(cached_keys.shape[1], dtype=jnp.int32)[None, :] < lengths[:, None]
    cached = jnp.where(valid[None, :, None, :], cached, MASKED)
    recent = (
        jnp.einsum("srgd,ird->srgi", query_group, new_keys, preferred_element_type=jnp.float32)
        * scale
    )
    decode_step_count = new_keys.shape[0]
    order_ok = (
        jnp.arange(decode_step_count)[None, :] <= jnp.arange(decode_step_count)[:, None]
    ) & True
    recent = jnp.where(order_ok[:, None, None, :], recent, MASKED)
    return (cached, recent)


def block_max(cached, recent):
    return jnp.maximum(
        jnp.max(cached, axis=-1, keepdims=True), jnp.max(recent, axis=-1, keepdims=True)
    )


def weigh(cached, recent, top, cached_vals, new_vals):
    e_cached = jnp.exp(cached - top)
    e_recent = jnp.exp(recent - top)
    total = jnp.sum(e_cached, axis=-1, keepdims=True) + jnp.sum(e_recent, axis=-1, keepdims=True)
    acc = jnp.einsum(
        "srgj,rjd->srgd",
        e_cached.astype(jnp.bfloat16),
        cached_vals,
        preferred_element_type=jnp.float32,
    )
    acc = acc + jnp.einsum(
        "srgi,ird->srgd",
        e_recent.astype(jnp.bfloat16),
        new_vals,
        preferred_element_type=jnp.float32,
    )
    return (acc, total)


def attend_whole(query_vectors, cached_keys, cached_vals, new_keys, new_vals, lengths):
    cached, recent = score_block(query_vectors, cached_keys, new_keys, lengths)
    top = block_max(cached, recent)
    acc, total = weigh(cached, recent, top, cached_vals, new_vals)
    return acc / total


def local(
    inputs,
    query_weight,
    key_value_weight,
    key_value_cache,
    lengths,
    request_adapter,
    adapter_storage_row,
    adapter_down_factors,
    adapter_up_factors,
):
    decode_step_count, request_count, model_width = inputs.shape
    tensor_count = lax.axis_size("tensor")
    pool_count = lax.axis_size("pool")
    tens_index = lax.axis_index("tensor")
    owner_count = tensor_count * pool_count
    head_width = key_value_cache.shape[-1]
    kv_split = 2 * head_width // key_value_weight.shape[1]
    portion_width = model_width // tensor_count
    query_columns = query_weight.shape[1]
    heads_present = query_columns // head_width
    adapter_count = adapter_down_factors.shape[0]
    table_len = adapter_storage_row.shape[0]
    matches = request_adapter[:, None] == jnp.arange(table_len, dtype=jnp.int32)[None, :]
    storage_rows = jnp.sum(jnp.where(matches, adapter_storage_row[None, :], 0), axis=1)
    owner_of = storage_rows // adapter_count
    local_row = storage_rows % adapter_count
    inputs_here = lax.dynamic_slice_in_dim(inputs, tens_index * portion_width, portion_width, 2)
    capacity = max(2, 2 * request_count // owner_count)
    ahead_mask = jnp.arange(request_count)[:, None] > jnp.arange(request_count)[None, :]
    place_in = jnp.sum((owner_of[:, None] == owner_of[None, :]) & ahead_mask, axis=1)
    target = owner_of * capacity + place_in
    hits = target[:, None] == jnp.arange(owner_count * capacity, dtype=jnp.int32)[None, :]
    wanted = jnp.sum(jnp.where(hits, local_row[:, None], 0), axis=0).reshape(owner_count, capacity)
    sent_states = jnp.einsum(
        "rk,srd->ksd", hits.astype(jnp.bfloat16), inputs_here, preferred_element_type=jnp.float32
    ).astype(jnp.bfloat16)
    sent_states = sent_states.reshape(owner_count, capacity, decode_step_count, portion_width)
    got_rows = lax.all_to_all(wanted, ("tensor", "pool"), split_axis=0, concat_axis=0, tiled=True)
    got_states = lax.all_to_all(
        sent_states, ("tensor", "pool"), split_axis=0, concat_axis=0, tiled=True
    )
    slots = got_rows.shape[1]
    rows_for = got_rows.reshape(tensor_count, pool_count, slots)[0]
    whole_states = got_states.reshape(
        tensor_count, pool_count, slots, decode_step_count, portion_width
    )
    whole_states = whole_states.transpose(1, 2, 3, 0, 4).reshape(
        pool_count, slots, decode_step_count, model_width
    )
    low = jnp.einsum(
        "pcsd,pckd->pcsk",
        whole_states,
        adapter_down_factors[rows_for],
        preferred_element_type=jnp.float32,
    ).astype(jnp.bfloat16)
    term = jnp.einsum(
        "pcsk,pckq->pcsq", low, adapter_up_factors[rows_for], preferred_element_type=jnp.float32
    )
    qslice = term.shape[3] // tensor_count
    outgoing = term.reshape(pool_count, slots, decode_step_count, tensor_count, qslice).transpose(
        3, 0, 1, 2, 4
    )
    outgoing = outgoing.reshape(owner_count, slots, decode_step_count, qslice)
    returned_terms = lax.all_to_all(
        outgoing, ("tensor", "pool"), split_axis=0, concat_axis=0, tiled=True
    )
    adapter_correction = returned_terms.reshape(
        owner_count * capacity, decode_step_count, query_columns
    )[target].transpose(1, 0, 2)
    flat = inputs.reshape(decode_step_count * request_count, model_width)
    projected_rows = jnp.dot(flat, query_weight, preferred_element_type=jnp.float32).reshape(
        decode_step_count, request_count, query_columns
    )
    positions = lengths[None, :] + jnp.arange(decode_step_count, dtype=jnp.int32)[:, None]
    query_vectors = (projected_rows + ADAPTER_SCALE * adapter_correction).reshape(
        decode_step_count, request_count, heads_present, head_width
    )
    query_vectors = rotate(query_vectors, positions[:, :, None]).astype(jnp.bfloat16)
    fresh_kv = jnp.dot(flat, key_value_weight, preferred_element_type=jnp.float32).reshape(
        decode_step_count, request_count, key_value_weight.shape[1]
    )
    is_first = tens_index % 2 == 0
    own_piece = jnp.where(is_first, rotate(fresh_kv, positions), fresh_kv).astype(jnp.bfloat16)
    other_piece = swapped(own_piece, "tensor", 0)
    new_keys = jnp.where(is_first, own_piece, other_piece)
    new_vals = jnp.where(is_first, other_piece, own_piece)
    own_cache = key_value_cache[:, 0]
    part_index = tens_index % kv_split
    other_cache = swapped(own_cache, "tensor", 0)
    leading = jnp.where(part_index == 0, own_cache, other_cache)
    trailing = jnp.where(part_index == 0, other_cache, own_cache)
    whole_cache = jnp.concatenate([leading, trailing], axis=2)
    attended = attend_whole(
        query_vectors, whole_cache[:, 0], whole_cache[:, 1], new_keys, new_vals, lengths
    )
    return attended.astype(jnp.bfloat16).reshape(decode_step_count, request_count, query_columns)


def solution(mesh):
    placed = (
        P(None, ("groups", "pool"), None),
        P(None, "tensor"),
        P(None, "tensor"),
        P(("groups", "pool"), "tensor", None, None, None),
        P(("groups", "pool")),
        P(("groups", "pool")),
        P("groups"),
        P(("groups", "tensor", "pool"), None, None),
        P(("groups", "tensor", "pool"), None, None),
    )
    return jax.shard_map(
        local,
        mesh=mesh,
        in_specs=placed,
        out_specs=P(None, ("groups", "pool"), "tensor"),
        check_vma=False,
    )
```

profile of v0, /device:TPU:0, one launch (start us, length us, event | category | flops | bytes accessed | tf_op | source)
XLA Modules:
  0.0 152.7 jit_solution(16172236704553321818)
XLA Ops:
  0.0 1.0 select_reduce_fusion
  2.0 7.4 %all-to-all-start.1 = ((s32[16,1,8]{2,1,0:T(1,128)}), s32[16,1,8]{2,1,0:T(1,128)S(1)}, u32[]{:S(2)}, u32[]{:S(2)}) async-start(s32[16,1,8]{2,1,0:T(1,128)} %bitcast.12), calls=%async_computation.1 | async-start | bytes 16384 | tf_op jit(solution)/shard_map/all_to_all | solution.py:120
  9.9 0.9 copy.59
  10.7 5.0 %all-to-all-done.1 = s32[16,1,8]{2,1,0:T(1,128)S(1)} async-done(((s32[16,1,8]{2,1,0:T(1,128)}), s32[16,1,8]{2,1,0:T(1,128)S(1)}, u32[]{:S(2)}, u32[]{:S(2)}) %all-to-all-start.1) | async-done | bytes 544 | tf_op jit(solution)/shard_map/all_to_all | solution.py:120
  15.8 3.6 %all-to-all-start = ((bf16[16,8,2,1024]{3,1,2,0:T(8,128)(2,1)}), bf16[16,8,2,1024]{3,1,2,0:T(8,128)(2,1)S(1)}, u32[]{:S(2)}, u32[]{:S(2)}) async-start(bf16[16,8,2,1024]{3,1,2,0:T(8,128)(2,1)} %copy.59), calls=%async_computation | async-start | bytes 1048576 | tf_op jit(solution)/shard_map/all_to_all | solution.py:121
  19.3 4.8 %copy.104 = bf16[64,1,2,128,128]{4,3,0,2,1:T(8,128)(2,1)} copy(bf16[64,1,2,128,128]{4,3,2,1,0:T(8,128)(2,1)} %param.12) | data formatting | bytes 8388608 | tf_op args[3]
  24.2 1.8 %collective-permute-start = (bf16[64,2,128,128]{3,2,0,1:T(8,128)(2,1)}, bf16[64,2,128,128]{3,2,0,1:T(8,128)(2,1)}, u32[]{:S(2)}, u32[]{:S(2)}) collective-permute-start(bf16[64,2,128,128]{3,2,0,1:T(8,128)(2,1)} %bitcast.109), channel_id=1, source_target_pairs={{0,2},{2,0},{4,6},{6,4},{8,10},{10,8},{12,14},{14,12},{1,3},{3,1},... | collective-permute-start | bytes 12582920 | tf_op jit(solution)/shard_map/ppermute | solution.py:14
  26.1 12.9 %gather_fusion.1 = bf16[16,64,8192]{2,1,0:T(8,128)(2,1)} fusion(bf16[16,64,8192]{2,1,0:T(8,128)(2,1)} %param.17, s32[1024]{0:T(1024)S(1)} %pad_clamp_fusion.1), kind=kCustom, calls=%fused_computation.1 | custom fusion | bytes 33554496 | tf_op jit(solution)/shard_map/gather | solution.py:139
  39.0 12.9 %gather_fusion = bf16[16,64,8192]{2,1,0:T(8,128)(2,1)} fusion(bf16[16,64,8192]{2,1,0:T(8,128)(2,1)} %param.16, s32[1024]{0:T(1024)S(1)} %pad_clamp_fusion.1), kind=kCustom, calls=%fused_computation | custom fusion | bytes 33554496 | tf_op jit(solution)/shard_map/gather | solution.py:135
  52.3 1.2 reshape.307
  53.5 14.1 %fusion.33 = f32[2,8,2,8192]{3,2,1,0:T(2,128)S(1)} fusion(bf16[2,8,64,8192]{3,2,1,0:T(8,128)(2,1)} %bitcast.110, bf16[2,8,2,8192]{3,2,1,0:T(2,128)(2,1)} %reshape.307, bf16[2,8,64,8192]{3,2,1,0:T(8,128)(2,1)} %bitcast.111), kind=kOutput, calls=%fused_computation.31 | convolution fusion | flops 67110912 | bytes 35127296 | tf_op jit(solution)/shard_map/pcsk,pckq->pcsq/dot_general | solution.py:138
  67.5 1.9 %reshape.269 = f32[2,8,2,8,1024]{4,3,2,1,0:T(8,128)} reshape(f32[2,8,2,8192]{3,2,1,0:T(2,128)S(1)} %fusion.33) | data formatting | bytes 2097152 | tf_op jit(solution)/shard_map/reshape | solution.py:142
  69.4 2.9 %copy.63 = f32[2,8,2,8,1024]{4,1,2,0,3:T(8,128)} copy(f32[2,8,2,8,1024]{4,3,2,1,0:T(8,128)} %reshape.269) | data formatting | bytes 2097152 | tf_op jit(solution)/shard_map/reshape | solution.py:142
  72.3 4.7 %all-to-all-start.2 = ((f32[16,8,2,1024]{3,1,2,0:T(8,128)}), f32[16,8,2,1024]{3,1,2,0:T(8,128)S(1)}, u32[]{:S(2)}, u32[]{:S(2)}) async-start(f32[16,8,2,1024]{3,1,2,0:T(8,128)} %bitcast.113), calls=%async_computation.2 | async-start | bytes 2097152 | tf_op jit(solution)/shard_map/all_to_all | solution.py:146
  77.0 2.3 %fusion.10 = f32[2,64,128]{2,1,0:T(8,128)S(1)} fusion(bf16[2,64,8192]{2,1,0:T(8,128)(2,1)S(1)} %copy-done, bf16[8192,128]{1,0:T(8,128)(2,1)} %param.11), kind=kOutput, calls=%fused_computation.17 | convolution fusion | flops 268435456 | bytes 4259840 | tf_op jit(solution)/shard_map/dot_general | solution.py:161
  79.7 2.0 %collective-permute-start.1 = (bf16[2,64,128]{2,1,0:T(8,128)(2,1)S(1)}, bf16[2,64,128]{2,1,0:T(8,128)(2,1)S(1)}, u32[]{:S(2)}, u32[]{:S(2)}) collective-permute-start(bf16[2,64,128]{2,1,0:T(8,128)(2,1)S(1)} %fusion.49), channel_id=1, source_target_pairs={{0,2},{2,0},{4,6},{6,4},{8,10},{10,8},{12,14},{14,12},{1,3},{3,1},... | collective-permute-start | bytes 98312 | tf_op jit(solution)/shard_map/ppermute | solution.py:14
  82.3 49.1 %collective-permute-done.1 = bf16[2,64,128]{2,1,0:T(8,128)(2,1)S(1)} collective-permute-done((bf16[2,64,128]{2,1,0:T(8,128)(2,1)S(1)}, bf16[2,64,128]{2,1,0:T(8,128)(2,1)S(1)}, u32[]{:S(2)}, u32[]{:S(2)}) %collective-permute-start.1) | collective-permute-done | bytes 32800 | tf_op jit(solution)/shard_map/ppermute | solution.py:14
  131.4 1.8 %copy.64 = f32[16,8,2,1024]{3,2,1,0:T(2,128)} copy(f32[16,8,2,1024]{3,1,2,0:T(8,128)S(1)} %all-to-all-done.2) | data formatting | bytes 2097152 | tf_op jit(solution)/shard_map/all_to_all | solution.py:146
  133.2 2.3 %gather_fusion.2 = f32[64,2,1024]{2,1,0:T(2,128)S(1)} fusion(f32[128,2,1024]{2,1,0:T(2,128)} %bitcast.114, s32[1024]{0:T(1024)S(1)} %pad_clamp_fusion), kind=kCustom, calls=%fused_computation.2 | custom fusion | bytes 1048832 | tf_op jit(solution)/shard_map/gather | solution.py:149
  135.5 8.2 %fusion.28 = f32[2,64,1024]{2,1,0:T(8,128)S(1)} fusion(bf16[2,64,8192]{2,1,0:T(8,128)(2,1)S(1)} %copy-done, bf16[8192,1024]{1,0:T(8,128)(2,1)} %param.10, f32[64,2,1024]{2,1,0:T(2,128)S(1)} %gather_fusion.2), kind=kOutput, calls=%fused_computation.26 | convolution fusion | flops 2147745792 | bytes 19922944 | tf_op jit(solution)/shard_map/dot_general | solution.py:153
  144.2 1.4 fusion.64
  145.9 2.5 %broadcast_select_fusion.1 = (bf16[64,2,128,128]{3,2,0,1:T(8,128)(2,1)S(1)}, bf16[64,2,128,128]{3,2,0,1:T(8,128)(2,1)S(1)}) fusion(bf16[64,2,128,128]{3,2,0,1:T(8,128)(2,1)} %collective-permute-done, pred[]{:T(512)S(6)} %eq.22, bf16[64,1,2,128,128]{4,3,2,1,0:T(8,128)(2,1)S(1)} %copy-done.1), kind=kLoop, calls=%fused_computation.16 | loop fusion | flops 4194304 | bytes 16777216 | tf_op jit(solution)/shard_map/jit(_where)/select_n | solution.py:172
  148.4 1.4 fusion.63
  150.9 0.9 fusion.37
  (42 shorter events, 5.4 us)
Async XLA Ops:
  0.0 9.4 %copy-start = (bf16[2,64,8192]{2,1,0:T(8,128)(2,1)S(1)}, bf16[2,64,8192]{2,1,0:T(8,128)(2,1)}, u32[]{:S(2)}) copy-start(bf16[2,64,8192]{2,1,0:T(8,128)(2,1)} %param.9) | copy-start | bytes 6291460
  2.0 13.7 %all-to-all-start.1 = ((s32[16,1,8]{2,1,0:T(1,128)}), s32[16,1,8]{2,1,0:T(1,128)S(1)}, u32[]{:S(2)}, u32[]{:S(2)}) async-start(s32[16,1,8]{2,1,0:T(1,128)} %bitcast.12), calls=%async_computation.1 | async-start | bytes 16384 | tf_op jit(solution)/shard_map/all_to_all | solution.py:120
  15.8 36.2 %all-to-all-start = ((bf16[16,8,2,1024]{3,1,2,0:T(8,128)(2,1)}), bf16[16,8,2,1024]{3,1,2,0:T(8,128)(2,1)S(1)}, u32[]{:S(2)}, u32[]{:S(2)}) async-start(bf16[16,8,2,1024]{3,1,2,0:T(8,128)(2,1)} %copy.59), calls=%async_computation | async-start | bytes 1048576 | tf_op jit(solution)/shard_map/all_to_all | solution.py:121
  19.3 6.6 %copy-start.2 = (s32[64]{0:T(128)S(1)}, s32[64]{0:T(128)}, u32[]{:S(2)}) copy-start(s32[64]{0:T(128)} %param.13) | copy-start | bytes 772
  24.2 121.4 %collective-permute-start = (bf16[64,2,128,128]{3,2,0,1:T(8,128)(2,1)}, bf16[64,2,128,128]{3,2,0,1:T(8,128)(2,1)}, u32[]{:S(2)}, u32[]{:S(2)}) collective-permute-start(bf16[64,2,128,128]{3,2,0,1:T(8,128)(2,1)} %bitcast.109), channel_id=1, source_target_pairs={{0,2},{2,0},{4,6},{6,4},{8,10},{10,8},{12,14},{14,12},{1,3},{3,1},... | collective-permute-start | bytes 12582920 | tf_op jit(solution)/shard_map/ppermute | solution.py:14
  72.3 59.1 %all-to-all-start.2 = ((f32[16,8,2,1024]{3,1,2,0:T(8,128)}), f32[16,8,2,1024]{3,1,2,0:T(8,128)S(1)}, u32[]{:S(2)}, u32[]{:S(2)}) async-start(f32[16,8,2,1024]{3,1,2,0:T(8,128)} %bitcast.113), calls=%async_computation.2 | async-start | bytes 2097152 | tf_op jit(solution)/shard_map/all_to_all | solution.py:146
  79.7 51.6 %collective-permute-start.1 = (bf16[2,64,128]{2,1,0:T(8,128)(2,1)S(1)}, bf16[2,64,128]{2,1,0:T(8,128)(2,1)S(1)}, u32[]{:S(2)}, u32[]{:S(2)}) collective-permute-start(bf16[2,64,128]{2,1,0:T(8,128)(2,1)S(1)} %fusion.49), channel_id=1, source_target_pairs={{0,2},{2,0},{4,6},{6,4},{8,10},{10,8},{12,14},{14,12},{1,3},{3,1},... | collective-permute-start | bytes 98312 | tf_op jit(solution)/shard_map/ppermute | solution.py:14
  143.7 2.2 %copy-start.1 = (bf16[64,1,2,128,128]{4,3,2,1,0:T(8,128)(2,1)S(1)}, bf16[64,1,2,128,128]{4,3,2,1,0:T(8,128)(2,1)}, u32[]{:S(2)}) copy-start(bf16[64,1,2,128,128]{4,3,2,1,0:T(8,128)(2,1)} %param.12) | copy-start | bytes 12582916
where the time goes:
time: 153 us
  waiting for transfers between devices  54.1 us (35%)
  local copies, waits for them, and re-layouts  44.3 us (29%)
  matrix products  28.9 us (19%)
  starting transfers between devices  19.5 us (13%)
  other arithmetic  5.57 us (4%)
    ppermute x2, waiting for transfers between devices, swapped(): return lax.ppermute(value, axis, pairs)  49.1 us
    dot_general x1, matrix products, local(): jnp.einsum('pcsk,pckq->pcsq', low, adapter_up_factors[rows_for], preferre...  14.1 us
    gather x1, local copies, waits for them, and re-layouts, local(): adapter_up_factors[rows_for]  12.9 us
    gather x1, local copies, waits for them, and re-layouts, local(): adapter_down_factors[rows_for]  12.9 us
    dot_general x1, matrix products, local(): jnp.dot(flat, query_weight, preferred_element_type=jnp.float32)  8.19 us
    all_to_all x1, starting transfers between devices, local(): lax.all_to_all(wanted, ('tensor', 'pool'), split_axis=0, concat_axis=0, t...  7.39 us
    unnamed x8, local copies, waits for them, and re-layouts  5.29 us
    all_to_all x1, waiting for transfers between devices, local(): lax.all_to_all(wanted, ('tensor', 'pool'), split_axis=0, concat_axis=0, t...  5.04 us
  transfers between devices with their start and end apart: 5, of which 2 were waited for; matrix products, arithmetic and copies ran while one was open for 46% of the time, Pallas kernels for 0%

commit v1 on v0

v1 whole, which is shorter than its diff:
```python
import functools

import jax
import jax.numpy as jnp
import numpy as np
from jax import lax
from jax.experimental import pallas as pl
from jax.experimental.pallas import tpu as pltpu
from jax.sharding import PartitionSpec as P

ROPE_BASE = 500000.0
ADAPTER_SCALE = 0.5
MASKED = -1e30
BF = jnp.bfloat16
F32 = jnp.float32
I32 = jnp.int32


def swapped(value, axis, bit):
    mask = 2**bit
    pairs = [(source, source ^ mask) for source in range(lax.axis_size(axis))]
    return lax.ppermute(value, axis, pairs)


def iota(shape, axis):
    return lax.broadcasted_iota(I32, shape, axis)


def column_of(row):
    count = row.shape[1]
    eye = iota((count, count), 0) == iota((count, count), 1)
    return jnp.sum(jnp.where(eye, row, jnp.zeros_like(row)), axis=1, keepdims=True)


def row_of(column):
    count = column.shape[0]
    eye = iota((count, count), 0) == iota((count, count), 1)
    return jnp.sum(jnp.where(eye, column, jnp.zeros_like(column)), axis=0, keepdims=True)


def routes(adapters, table, per_owner):
    requests = adapters.shape[1]
    rows = table.shape[1]
    match = (iota((rows, requests), 0) == adapters).astype(F32)
    stored = jnp.dot(
        table.astype(F32), match, precision=lax.Precision.HIGHEST, preferred_element_type=F32
    ).astype(I32)
    owner = stored // per_owner
    local_row = stored - owner * per_owner
    owner_column = column_of(owner)
    ahead = iota((requests, requests), 0) < iota((requests, requests), 1)
    place = jnp.sum(
        jnp.where((owner_column == owner) & ahead, 1, 0), axis=0, keepdims=True
    )
    return owner, local_row, place


def stage_kernel(states_hbm, down_hbm, adapters_hbm, table_hbm, *rest):
    states, down, adapters, table, sem, other_sem = rest
    parts = sem.shape[0]
    size = down.shape[0] // parts
    copies = [
        pltpu.make_async_copy(states_hbm, states, other_sem.at[0]),
        pltpu.make_async_copy(adapters_hbm, adapters, other_sem.at[1]),
        pltpu.make_async_copy(table_hbm, table, other_sem.at[2]),
    ]
    for part in range(parts):
        span = pl.ds(part * size, size)
        copies.append(pltpu.make_async_copy(down_hbm.at[span], down.at[span], sem.at[part]))
    for copy in copies:
        copy.start()
    for copy in copies:
        copy.wait()


def lora_kernel(
    dims,
    own_ref,
    other_ref,
    own_adapters_ref,
    other_adapters_ref,
    table_ref,
    down,
    down_hbm,
    up_hbm,
    out_ref,
    down_rest,
    up,
    chosen,
    low,
    down_sem,
    up_sem,
):
    steps, requests, capacity, per_owner, rank, tensor_count, pool_count = dims
    here_rows = down.shape[0]
    down_rows = down_rest.shape[0]
    up_parts = up_sem.shape[0]
    up_columns = up.shape[1] // up_parts
    rest_copy = pltpu.make_async_copy(
        down_hbm.at[pl.ds(here_rows, down_rows)], down_rest, down_sem.at[0]
    )

    def up_copy(part):
        columns = pl.ds(pl.multiple_of(part * up_columns, up_columns), up_columns)
        return pltpu.make_async_copy(
            up_hbm.at[:, columns], up.at[:, columns], up_sem.at[part]
        )

    rest_copy.start()

    @pl.loop(0, up_parts)
    def _(part):
        up_copy(part).start()

    pool = lax.axis_index("pool")
    me = lax.axis_index("tensor") * pool_count + pool
    table = table_ref[...]
    rows = steps * capacity
    local_rows = []
    for which, (states_ref, adapters_ref) in enumerate(
        ((own_ref, own_adapters_ref), (other_ref, other_adapters_ref))
    ):
        owner, local_row, place = routes(adapters_ref[...], table, per_owner)
        owner = jnp.concatenate([owner] * steps, axis=1)
        place = jnp.concatenate([place] * steps, axis=1)
        local_row = jnp.concatenate([local_row] * steps, axis=1)
        shape = (rows, steps * requests)
        row = iota(shape, 0)
        row_step = row // capacity
        hit = (
            (owner == me)
            & (place == row - row_step * capacity)
            & (row_step == iota(shape, 1) // requests)
        )
        local_rows.append(jnp.sum(jnp.where(hit, local_row, 0), axis=1, keepdims=True))
        pick = jnp.where(hit, 1.0, 0.0).astype(BF)
        chosen[which] = jnp.dot(
            pick, states_ref[...], preferred_element_type=F32
        ).astype(BF)
    local_rows = jnp.concatenate(local_rows, axis=0)
    states = jnp.concatenate([chosen[0], chosen[1]], axis=0)

    def factors_of(rows_ref, first_row):
        count = rows_ref.shape[0]
        piece = lax.dot_general(
            rows_ref[...], states, (((1,), (1,)), ((), ())), preferred_element_type=F32
        ).T
        holder = (iota(piece.shape, 1) + first_row) // rank
        low[:, pl.ds(first_row, count)] = jnp.where(
            holder == local_rows, piece.astype(BF), jnp.zeros(piece.shape, BF)
        )

    for first_row in range(0, here_rows, down_rows):
        factors_of(down.at[pl.ds(first_row, down_rows)], first_row)

    @pl.loop(0, 1)
    def _(_):
        rest_copy.wait()

    factors_of(down_rest, here_rows)

    @pl.loop(0, up_parts)
    def _(part):
        up_copy(part).wait()
        columns = pl.ds(pl.multiple_of(part * up_columns, up_columns), up_columns)
        term = jnp.dot(low[...], up[:, columns], preferred_element_type=F32).astype(BF)
        out_ref[part * pool_count + pool] = term[:rows]
        out_ref[part * pool_count + 1 - pool] = term[rows:]


def project_kernel(
    dims,
    states_ref,
    adapters_ref,
    table_ref,
    lengths_ref,
    freq_ref,
    weight_hbm,
    new_weight_hbm,
    out_ref,
    piece_ref,
    cosine_ref,
    sine_ref,
    spread_ref,
    weight,
    new_weight,
    sem,
):
    steps, requests, capacity, per_owner = dims
    parts = sem.shape[0] - 1
    depth = weight.shape[0] // parts
    new_copy = pltpu.make_async_copy(new_weight_hbm, new_weight, sem.at[parts])

    def part_copy(part):
        span = pl.ds(pl.multiple_of(part * depth, depth), depth)
        return pltpu.make_async_copy(weight_hbm.at[span], weight.at[span], sem.at[part])

    @pl.loop(0, parts)
    def _(part):
        part_copy(part).start()

    new_copy.start()

    rows = steps * capacity
    owner, _, place = routes(adapters_ref[...], table_ref[...], per_owner)
    owner = jnp.concatenate([column_of(owner)] * steps, axis=0)
    place = jnp.concatenate([column_of(place)] * steps, axis=0)
    shape = spread_ref.shape
    slot = iota(shape, 1)
    slot_owner = slot // rows
    slot_step = (slot - slot_owner * rows) // capacity
    slot_place = slot - slot_owner * rows - slot_step * capacity
    hit = (
        (slot_owner == owner)
        & (slot_place == place)
        & (slot_step == iota(shape, 0) // requests)
    )
    spread_ref[...] = jnp.where(hit, 1.0, 0.0).astype(BF)

    length = column_of(lengths_ref[...])
    position = jnp.concatenate([length + step for step in range(steps)], axis=0)
    angle = position.astype(F32) * freq_ref[...]
    cosine = jnp.cos(angle)
    sine = jnp.sin(angle)
    half = angle.shape[1] // 2
    sine = jnp.where(iota(angle.shape, 1) < half, -sine, sine)
    cosine_ref[...] = cosine
    sine_ref[...] = sine

    out_ref[...] = jnp.zeros_like(out_ref)

    @pl.loop(0, parts)
    def _(part):
        part_copy(part).wait()
        span = pl.ds(pl.multiple_of(part * depth, depth), depth)
        out_ref[...] += jnp.dot(
            states_ref[:, span], weight[span, :], preferred_element_type=F32
        )

    new_copy.wait()
    fresh = jnp.dot(states_ref[...], new_weight[...], preferred_element_type=F32)
    turned = fresh * cosine_ref[...] + pltpu.roll(fresh, half, 1) * sine_ref[...]
    is_first = lax.axis_index("tensor") % 2 == 0
    piece_ref[...] = jnp.where(is_first, turned, fresh).astype(BF)


def load_kernel(source, after, out_ref, sem):
    copy = pltpu.make_async_copy(source, out_ref, sem.at[0])
    copy.start()
    copy.wait()


def query_kernel(
    dims, terms_ref, spread_ref, projected_ref, piece_ref, cosine_ref, sine_ref, out_ref, packed
):
    steps, requests, heads, head_width = dims
    correction = jnp.dot(spread_ref[...], terms_ref[...], preferred_element_type=F32)
    query = projected_ref[...] + ADAPTER_SCALE * correction
    cosine = cosine_ref[...]
    sine = sine_ref[...]
    count = packed.shape[0]
    for head in range(heads):
        vector = query[:, head * head_width : (head + 1) * head_width]
        vector = vector * cosine + pltpu.roll(vector, head_width // 2, 1) * sine
        for step in range(steps):
            packed[pl.ds(step * heads + head, requests, stride=steps * heads), :] = vector[
                step * requests : (step + 1) * requests
            ]
    out_ref[:count, :] = packed[...].astype(BF)
    out_ref[count:, :] = piece_ref[...]


def attend(dims, lengths_ref, query_ref, cache_ref, keys, vals, scratch, store):
    steps, requests, heads, head_width, kv_split = dims
    scores_ref, recent_ref, weights_ref, new_weights_ref, acc_ref = scratch
    per_request = steps * heads
    count = requests * per_request
    scale = head_width ** (-0.5)
    context = cache_ref.shape[2]
    part = lax.axis_index("tensor") % kv_split
    base = part * context
    lane = iota((per_request, context), 1)
    for request in range(requests):
        span = pl.ds(request * per_request, per_request)
        score = lax.dot_general(
            query_ref[span, :],
            cache_ref[request, 0],
            (((1,), (1,)), ((), ())),
            preferred_element_type=F32,
        )
        scores_ref[span, :] = jnp.where(
            lane < lengths_ref[request] - base, score * scale, MASKED
        )
    rows = min(128, count)
    shape = (rows, steps * requests)
    column_step = iota(shape, 1) // requests
    column_request = iota(shape, 1) - column_step * requests
    row_request = iota(shape, 0) // per_request
    row_step = (iota(shape, 0) - row_request * per_request) // heads
    allowed = (column_step <= row_step) & (part == 0)
    ahead = column_request - row_request
    for at in range(count // rows):
        span = pl.ds(at * rows, rows)
        recent = lax.dot_general(
            query_ref[span, :], keys, (((1,), (1,)), ((), ())), preferred_element_type=F32
        )
        recent_ref[span, :] = jnp.where(
            allowed & (ahead == at * (rows // per_request)), recent * scale, MASKED
        )
    totals = []
    for at in range(count // rows):
        span = pl.ds(at * rows, rows)
        scores = scores_ref[span, :]
        recent = recent_ref[span, :]
        top = jnp.maximum(
            jnp.max(scores, axis=1, keepdims=True), jnp.max(recent, axis=1, keepdims=True)
        ) if scores.shape != recent.shape else jnp.max(
            jnp.maximum(scores, recent), axis=1, keepdims=True
        )
        e_cached = jnp.exp(scores - top)
        e_recent = jnp.exp(recent - top)
        total = (
            jnp.sum(e_cached, axis=1, keepdims=True) + jnp.sum(e_recent, axis=1, keepdims=True)
            if scores.shape != recent.shape
            else jnp.sum(e_cached + e_recent, axis=1, keepdims=True)
        )
        weights_ref[span, :] = e_cached.astype(BF)
        new_weights_ref[span, :] = e_recent.astype(BF)
        totals.append((top, total))
    for request in range(requests):
        span = pl.ds(request * per_request, per_request)
        acc_ref[span, :] = jnp.dot(
            weights_ref[span, :], cache_ref[request, 1], preferred_element_type=F32
        )
    for at in range(count // rows):
        span = pl.ds(at * rows, rows)
        top, total = totals[at]
        acc = acc_ref[span, :] + jnp.dot(
            new_weights_ref[span, :], vals, preferred_element_type=F32
        )
        store(at, rows, acc * (1.0 / total), top + jnp.log(total))


def new_pieces(own, other):
    first = lax.axis_index("tensor") % 2 == 0
    keys = jnp.where(first, own.astype(F32), other.astype(F32)).astype(BF)
    vals = jnp.where(first, other.astype(F32), own.astype(F32)).astype(BF)
    return keys, vals


def own_kernel(dims, lengths_ref, sent_ref, got_ref, cache_ref, out_ref, level_ref, *scratch):
    count = out_ref.shape[0]
    keys, vals = new_pieces(sent_ref[count:, :], got_ref[count:, :])

    def store(at, rows, result, level):
        out_ref[pl.ds(at * rows, rows), :] = result
        level_ref[pl.ds(at * rows, rows), :] = level

    attend(dims, lengths_ref, sent_ref, cache_ref, keys, vals, scratch, store)


def send_kernel(dims, lengths_ref, sent_ref, got_ref, cache_ref, out_ref, levels, *scratch):
    lines = levels.shape[0]
    count = lines * 128
    keys, vals = new_pieces(sent_ref[count:, :], got_ref[count:, :])

    def store(at, rows, result, level):
        out_ref[pl.ds(at * rows, rows), :] = result.astype(BF)
        for line in range(rows // 128):
            levels[pl.ds(at * (rows // 128) + line, 1), :] = row_of(
                level[line * 128 : (line + 1) * 128]
            )

    attend(dims, lengths_ref, got_ref, cache_ref, keys, vals, scratch, store)
    rest = levels[...]
    pieces = []
    for _ in range(3):
        piece = rest.astype(BF)
        pieces.append(piece)
        rest = rest - piece.astype(F32)
    pieces.append(jnp.zeros_like(pieces[0]))
    out_ref[pl.ds(count, 4 * lines), :] = jnp.concatenate(pieces, axis=0)


def merge_kernel(dims, own_ref, level_ref, got_ref, out_ref, packed):
    steps, requests, heads, head_width = dims
    count = own_ref.shape[0]
    lines = count // 128
    extra = got_ref[pl.ds(count, 4 * lines), :].astype(F32)
    other_level = extra[:lines] + extra[lines : 2 * lines] + extra[2 * lines : 3 * lines]
    for line in range(lines):
        span = pl.ds(line * 128, 128)
        theirs = column_of(other_level[line : line + 1])
        mine = level_ref[span, :]
        top = jnp.maximum(mine, theirs)
        mine = jnp.exp(mine - top)
        theirs = jnp.exp(theirs - top)
        total = mine + theirs
        packed[span, :] = own_ref[span, :] * (mine / total) + got_ref[span, :].astype(F32) * (
            theirs / total
        )
    for step in range(steps):
        for head in range(heads):
            out_ref[
                step * requests : (step + 1) * requests,
                head * head_width : (head + 1) * head_width,
            ] = packed[pl.ds(step * heads + head, requests, stride=steps * heads), :].astype(BF)


def in_vmem(shape, dtype):
    return pltpu.VMEM(shape, dtype)


def in_hbm(value):
    return pltpu.with_memory_space_constraint(value, pltpu.HBM)


def vmem_limit(mebibytes):
    return pltpu.CompilerParams(vmem_limit_bytes=mebibytes * 2**20)


def whole(*refs):
    return [pl.BlockSpec(memory_space=pltpu.VMEM)] * len(refs)


def local(
    inputs,
    query_weight,
    key_value_weight,
    key_value_cache,
    lengths,
    request_adapter,
    adapter_storage_row,
    adapter_down_factors,
    adapter_up_factors,
):
    steps, requests, width = inputs.shape
    tensor_count = lax.axis_size("tensor")
    pool_count = lax.axis_size("pool")
    owners = tensor_count * pool_count
    head_width = key_value_cache.shape[-1]
    context = key_value_cache.shape[-2]
    kv_split = 2 * head_width // key_value_weight.shape[1]
    query_columns = query_weight.shape[1]
    heads = query_columns // head_width
    per_owner, rank, _ = adapter_down_factors.shape
    capacity = max(2, 2 * requests // owners)
    rows = steps * capacity
    count = steps * requests

    flat = inputs.reshape(count, width)
    adapters = request_adapter.reshape(1, requests)
    other_adapters = swapped(adapters, "pool", 0)
    other_flat = swapped(flat, "pool", 0)
    table = adapter_storage_row.reshape(1, -1)
    down = adapter_down_factors.reshape(per_owner * rank, width)
    up = adapter_up_factors.reshape(per_owner * rank, -1)
    cache = key_value_cache.reshape(requests, 2, context, head_width)
    anywhere = pl.BlockSpec(memory_space=pltpu.HBM)
    smem = pl.BlockSpec(memory_space=pltpu.SMEM)

    rest_rows = per_owner * rank // 4
    here_rows = per_owner * rank - rest_rows
    flat_here, down_here, adapters, table = pl.pallas_call(
        stage_kernel,
        out_shape=[
            in_vmem(flat.shape, BF),
            in_vmem((here_rows, width), BF),
            in_vmem(adapters.shape, I32),
            in_vmem(table.shape, I32),
        ],
        in_specs=[anywhere] * 4,
        out_specs=whole(*range(4)),
        scratch_shapes=[pltpu.SemaphoreType.DMA((3,)), pltpu.SemaphoreType.DMA((3,))],
        compiler_params=vmem_limit(4),
        cost_estimate=pl.CostEstimate(
            flops=0, bytes_accessed=2 * (down.size + flat.size), transcendentals=0
        ),
        name="stage",
    )(in_hbm(flat), in_hbm(down), in_hbm(adapters), in_hbm(table))

    lora_dims = (steps, requests, capacity, per_owner, rank, tensor_count, pool_count)
    outgoing = pl.pallas_call(
        functools.partial(lora_kernel, lora_dims),
        out_shape=jax.ShapeDtypeStruct((owners, rows, query_columns), BF),
        in_specs=whole(*range(6)) + [anywhere] * 2,
        out_specs=whole(0)[0],
        scratch_shapes=[
            pltpu.VMEM((rest_rows, width), BF),
            pltpu.VMEM(up.shape, BF),
            pltpu.VMEM((2, rows, width), BF),
            pltpu.VMEM((2 * rows, per_owner * rank), BF),
            pltpu.SemaphoreType.DMA((1,)),
            pltpu.SemaphoreType.DMA((tensor_count,)),
        ],
        compiler_params=vmem_limit(24),
        cost_estimate=pl.CostEstimate(
            flops=8 * rows * per_owner * rank * width,
            bytes_accessed=2 * per_owner * rank * width,
            transcendentals=0,
        ),
        name="lora",
    )(
        flat_here,
        pltpu.with_memory_space_constraint(other_flat, pltpu.VMEM),
        adapters,
        other_adapters,
        table,
        down_here,
        in_hbm(down),
        in_hbm(up),
    )
    terms = lax.all_to_all(outgoing, ("tensor", "pool"), split_axis=0, concat_axis=0, tiled=True)
    terms = terms.reshape(owners * rows, query_columns)

    flat_late, adapters, table, _ = lax.optimization_barrier(
        (flat_here, adapters, table, outgoing)
    )
    power = np.arange(head_width // 2, dtype=np.float64) * (-2.0 / head_width)
    freq = np.tile(ROPE_BASE**power, 2).astype(np.float32).reshape(1, head_width)
    projected, own_piece, cosine, sine, spread = pl.pallas_call(
        functools.partial(project_kernel, (steps, requests, capacity, per_owner)),
        out_shape=[
            in_vmem((count, query_columns), F32),
            in_vmem((count, head_width), BF),
            in_vmem((count, head_width), F32),
            in_vmem((count, head_width), F32),
            in_vmem((count, owners * rows), BF),
        ],
        in_specs=whole(*range(5)) + [anywhere] * 2,
        out_specs=whole(*range(5)),
        scratch_shapes=[
            pltpu.VMEM(query_weight.shape, BF),
            pltpu.VMEM(key_value_weight.shape, BF),
            pltpu.SemaphoreType.DMA((17,)),
        ],
        compiler_params=vmem_limit(24),
        cost_estimate=pl.CostEstimate(
            flops=2 * count * width * query_columns,
            bytes_accessed=2 * width * query_columns,
            transcendentals=0,
        ),
        name="project",
    )(
        flat_late,
        adapters,
        table,
        lengths.reshape(1, requests),
        jnp.asarray(freq),
        in_hbm(query_weight),
        in_hbm(key_value_weight),
    )

    dims = (steps, requests, heads, head_width)
    packed_rows = count * heads
    sent = pl.pallas_call(
        functools.partial(query_kernel, dims),
        out_shape=jax.ShapeDtypeStruct((packed_rows + count, head_width), BF),
        in_specs=whole(*range(6)),
        out_specs=whole(0)[0],
        scratch_shapes=[pltpu.VMEM((packed_rows, head_width), F32)],
        compiler_params=vmem_limit(8),
        name="query",
    )(terms, spread, projected, own_piece, cosine, sine)
    got = swapped(sent, "tensor", 0)

    cache_here = pl.pallas_call(
        load_kernel,
        out_shape=in_vmem(cache.shape, BF),
        in_specs=[anywhere, pl.BlockSpec(memory_space=pl.ANY)],
        out_specs=whole(0)[0],
        scratch_shapes=[pltpu.SemaphoreType.DMA((1,))],
        compiler_params=vmem_limit(1),
        cost_estimate=pl.CostEstimate(
            flops=0, bytes_accessed=4 * cache.size, transcendentals=0
        ),
        name="load",
    )(in_hbm(cache), sent)

    lines = packed_rows // 128
    attend_dims = (steps, requests, heads, head_width, kv_split)
    attend_scratch = [
        pltpu.VMEM((packed_rows, context), F32),
        pltpu.VMEM((packed_rows, count), F32),
        pltpu.VMEM((packed_rows, context), BF),
        pltpu.VMEM((packed_rows, count), BF),
        pltpu.VMEM((packed_rows, head_width), F32),
    ]
    cost = pl.CostEstimate(
        flops=4 * packed_rows * context * head_width,
        bytes_accessed=2 * cache.size,
        transcendentals=packed_rows * context,
    )
    sending = pl.pallas_call(
        functools.partial(send_kernel, attend_dims),
        out_shape=jax.ShapeDtypeStruct((packed_rows + 4 * lines, head_width), BF),
        in_specs=[smem] + whole(*range(3)),
        out_specs=whole(0)[0],
        scratch_shapes=[pltpu.VMEM((lines, 128), F32)] + attend_scratch,
        compiler_params=vmem_limit(12),
        cost_estimate=cost,
        name="send",
    )(lengths, sent, got, cache_here)
    partial = swapped(sending, "tensor", 0)
    own, level = pl.pallas_call(
        functools.partial(own_kernel, attend_dims),
        out_shape=[
            jax.ShapeDtypeStruct((packed_rows, head_width), F32),
            jax.ShapeDtypeStruct((packed_rows, 1), F32),
        ],
        in_specs=[smem] + whole(*range(3)),
        out_specs=whole(*range(2)),
        scratch_shapes=attend_scratch,
        compiler_params=vmem_limit(12),
        cost_estimate=cost,
        name="own",
    )(lengths, sent, got, cache_here)
    attended = pl.pallas_call(
        functools.partial(merge_kernel, dims),
        out_shape=jax.ShapeDtypeStruct((count, query_columns), BF),
        in_specs=whole(*range(3)),
        out_specs=whole(0)[0],
        scratch_shapes=[pltpu.VMEM((packed_rows, head_width), F32)],
        compiler_params=vmem_limit(8),
        name="merge",
    )(own, level, partial)
    return attended.reshape(steps, requests, query_columns)


def solution(mesh):
    placed = (
        P(None, ("groups", "pool"), None),
        P(None, "tensor"),
        P(None, "tensor"),
        P(("groups", "pool"), "tensor", None, None, None),
        P(("groups", "pool")),
        P(("groups", "pool")),
        P("groups"),
        P(("groups", "tensor", "pool"), None, None),
        P(("groups", "tensor", "pool"), None, None),
    )
    return jax.shard_map(
        local,
        mesh=mesh,
        in_specs=placed,
        out_specs=P(None, ("groups", "pool"), "tensor"),
        check_vma=False,
    )
```

time: 153 us -> 62.2 us (0.41)
  local copies, waits for them, and re-layouts: 44.3 us -> 0.01 us
  waiting for transfers between devices: 54.1 us -> 17 us
  Pallas kernels: 0 us -> 35.2 us
  matrix products: 28.9 us -> 0 us
  starting transfers between devices: 19.5 us -> 9.59 us
  other arithmetic: 5.57 us -> 0 us
    ppermute x2 -> x4, waiting for transfers between devices: 49.1 us -> 10.1 us  [swapped(): return lax.ppermute(value, axis, pairs)]
    pallas_call x0 -> x8, Pallas kernels: none -> 35.2 us  [the longest x1 12.8 us: local(): pl.pallas_call(functools.partial(lora_kernel, lora_dims), out_shape=jax.S...]
    dot_general x8 -> x0, matrix products: 28.9 us -> none  [the longest x1 14.1 us: local(): jnp.einsum('pcsk,pckq->pcsq', low, adapter_up_factors[rows_for], preferre...]
    gather x3 -> x0, local copies, waits for them, and re-layouts: 28.2 us -> none  [the longest x1 12.9 us: local(): adapter_up_factors[rows_for]]
    all_to_all x2 -> x0, starting transfers between devices: 11 us -> none  [the longest x1 7.39 us: local(): lax.all_to_all(wanted, ('tensor', 'pool'), split_axis=0, concat_axis=0, t...]
    reshape x7 -> x0, local copies, waits for them, and re-layouts: 7.92 us -> none  [the longest x2 4.76 us: local(): term.reshape(pool_count, slots, decode_step_count, tensor_count, qslice)]
    all_to_all x1, waiting for transfers between devices: 0.01 us -> 6.89 us  [local(): lax.all_to_all(outgoing, ('tensor', 'pool'), split_axis=0, concat_axis=0,...]
    unnamed x8 -> x4, local copies, waits for them, and re-layouts: 5.29 us -> 0.01 us
  transfers between devices with their start and end apart: 5 -> 5, of which waited for: 2 -> 3; matrix products, arithmetic and copies ran while one was open for 46% -> 0% of each run, Pallas kernels for 0% -> 29%
where the time goes in v1:
time: 62.2 us; the launch traced here: 61.9 us
  Pallas kernels  35.2 us (57%)
  waiting for transfers between devices  17 us (27%)
  starting transfers between devices  9.59 us (15%)
    pallas_call x1, Pallas kernels, local(): pl.pallas_call(functools.partial(lora_kernel, lora_dims), out_shape=jax.S...  12.8 us
    ppermute x4, waiting for transfers between devices, swapped(): return lax.ppermute(value, axis, pairs)  10.1 us
    pallas_call x1, Pallas kernels, local(): pl.pallas_call(functools.partial(project_kernel, (steps, requests, capaci...  7.55 us
    all_to_all x1, starting transfers between devices, local(): lax.all_to_all(outgoing, ('tensor', 'pool'), split_axis=0, concat_axis=0,...  7.4 us
    all_to_all x1, waiting for transfers between devices, local(): lax.all_to_all(outgoing, ('tensor', 'pool'), split_axis=0, concat_axis=0,...  6.89 us
    pallas_call x1, Pallas kernels, local(): pl.pallas_call(stage_kernel, out_shape=[in_vmem(flat.shape, BF), in_vmem(...  5.31 us
    pallas_call x1, Pallas kernels, local(): pl.pallas_call(functools.partial(send_kernel, attend_dims), out_shape=jax...  2.77 us
    pallas_call x1, Pallas kernels, local(): pl.pallas_call(functools.partial(own_kernel, attend_dims), out_shape=[jax...  2.76 us
  transfers between devices with their start and end apart: 5, of which 3 were waited for; matrix products, arithmetic and copies ran while one was open for 0% of the time, Pallas kernels for 29%

profile of v1, /device:TPU:0, one launch (start us, length us, event | category | flops | bytes accessed | tf_op | source)
XLA Modules:
  0.0 61.9 jit_solution(13865296102954199504)
XLA Ops:
  0.0 0.5 collective-permute-start
  0.5 0.1 collective-permute-start.1
  0.5 5.3 %stage.1 = (bf16[128,8192]{1,0:T(8,128)(2,1)S(1)}, bf16[768,8192]{1,0:T(8,128)(2,1)S(1)}, s32[1,64]{1,0:T(1,128)S(1)}, s32[1,256]{1,0:T(1,128)S(1)}) custom-call(bf16[128,8192]{1,0:T(8,128)(2,1)} %bitcast.16, bf16[1024,8192]{1,0:T(8,128)(2,1)} %bitcast.11, s32[1,64]{1,0:T(1,128)} %bitcast.19, s32[1,256]{1,0:T(1,128)} %bitcast.17), custom_call_target="tpu_custom_call" | custom-call | bytes 18874368 | tf_op jit(solution)/shard_map/stage/pallas_call | solution.py:464
  5.8 0.0 collective-permute-done.1.other_adapters_ref
  5.8 0.0 collective-permute-done.other_ref
  5.9 0.0 copy-start
  5.9 0.0 copy-start.1
  5.9 12.8 %lora.1 = bf16[16,16,1024]{2,1,0:T(8,128)(2,1)} custom-call(bf16[128,8192]{1,0:T(8,128)(2,1)S(1)} %get-tuple-element.23.own_ref.states_ref, bf16[128,8192]{1,0:T(8,128)(2,1)S(1)} %collective-permute-done.other_ref, s32[1,64]{1,0:T(1,128)S(1)} %get-tuple-element.24.own_adapters_ref.adapters_ref, s32[1,64]{1,0:T(1,128)S(1)} %collective-permute-done.1.other_adapters_ref, ...), custom_call_target="tpu_custom_call" | custom-call | flops 1073741824 | bytes 16777216 | tf_op jit(solution)/shard_map/lora/pallas_call | solution.py:483
  18.7 7.4 %all-to-all-start = ((bf16[16,16,1024]{2,1,0:T(8,128)(2,1)}), bf16[16,16,1024]{2,1,0:T(8,128)(2,1)S(1)}, u32[]{:S(2)}, u32[]{:S(2)}) async-start(bf16[16,16,1024]{2,1,0:T(8,128)(2,1)} %lora.1), calls=%async_computation | async-start | bytes 1048576 | tf_op jit(solution)/shard_map/all_to_all | solution.py:513
  26.1 0.0 copy-done
  26.1 0.0 copy-done.1
  26.1 7.6 %project.1 = (f32[128,1024]{1,0:T(8,128)S(1)}, bf16[128,128]{1,0:T(8,128)(2,1)S(1)}, f32[128,128]{1,0:T(8,128)S(1)}, f32[128,128]{1,0:T(8,128)S(1)}, bf16[128,256]{1,0:T(8,128)(2,1)S(1)}) custom-call(bf16[128,8192]{1,0:T(8,128)(2,1)S(1)} %get-tuple-element.23.own_ref.states_ref, s32[1,64]{1,0:T(1,128)S(1)} %get-tuple-element.24.own_adapters_ref.adapters_ref, ...), custom_call_target="tpu_custom_call" | custom-call | flops 2147483648 | bytes 16777216 | tf_op jit(solution)/shard_map/project/pallas_call | solution.py:521
  33.7 6.9 %all-to-all-done = bf16[16,16,1024]{2,1,0:T(8,128)(2,1)S(1)} async-done(((bf16[16,16,1024]{2,1,0:T(8,128)(2,1)}), bf16[16,16,1024]{2,1,0:T(8,128)(2,1)S(1)}, u32[]{:S(2)}, u32[]{:S(2)}) %all-to-all-start) | async-done | bytes 524320 | tf_op jit(solution)/shard_map/all_to_all | solution.py:513
  40.6 0.5 query.1.after.sent_ref
  41.0 0.5 collective-permute-start.2
  41.5 2.2 %load.1.cache_ref = bf16[64,2,128,128]{3,2,1,0:T(8,128)(2,1)S(1)} custom-call(bf16[64,2,128,128]{3,2,1,0:T(8,128)(2,1)} %bitcast.14, bf16[1152,128]{1,0:T(8,128)(2,1)S(1)} %query.1.after.sent_ref), custom_call_target="tpu_custom_call" | custom-call | bytes 8388608 | tf_op jit(solution)/shard_map/load/pallas_call | solution.py:567
  43.7 6.3 %collective-permute-done.2.got_ref = bf16[1152,128]{1,0:T(8,128)(2,1)S(1)} collective-permute-done((bf16[1152,128]{1,0:T(8,128)(2,1)S(1)}, bf16[1152,128]{1,0:T(8,128)(2,1)S(1)}, u32[]{:S(2)}, u32[]{:S(2)}) %collective-permute-start.2) | collective-permute-done | bytes 294944 | tf_op jit(solution)/shard_map/ppermute | solution.py:22
  50.0 2.8 %send.1 = bf16[1056,128]{1,0:T(8,128)(2,1)S(1)} custom-call(s32[64]{0:T(128)S(1)} %copy-done, bf16[1152,128]{1,0:T(8,128)(2,1)S(1)} %query.1.after.sent_ref, bf16[1152,128]{1,0:T(8,128)(2,1)S(1)} %collective-permute-done.2.got_ref, bf16[64,2,128,128]{3,2,1,0:T(8,128)(2,1)S(1)} %load.1.cache_ref), custom_call_target="tpu_custom_call" | custom-call | flops 67108864 | bytes 4194304 | tf_op jit(solution)/shard_map/send/pallas_call | solution.py:594
  52.8 1.2 %collective-permute-start.3 = (bf16[1056,128]{1,0:T(8,128)(2,1)S(1)}, bf16[1056,128]{1,0:T(8,128)(2,1)S(1)}, u32[]{:S(2)}, u32[]{:S(2)}) collective-permute-start(bf16[1056,128]{1,0:T(8,128)(2,1)S(1)} %send.1), channel_id=1, source_target_pairs={{0,2},{2,0},{4,6},{6,4},{8,10},{10,8},{12,14},{14,12},{1,3},{3,1},... | collective-permute-start | bytes 811016 | tf_op jit(solution)/shard_map/ppermute | solution.py:22
  54.0 2.8 %own.1 = (f32[1024,128]{1,0:T(8,128)S(1)}, f32[1024,1]{1,0:T(8,128)S(1)}) custom-call(s32[64]{0:T(128)S(1)} %copy-done, bf16[1152,128]{1,0:T(8,128)(2,1)S(1)} %query.1.after.sent_ref, bf16[1152,128]{1,0:T(8,128)(2,1)S(1)} %collective-permute-done.2.got_ref, bf16[64,2,128,128]{3,2,1,0:T(8,128)(2,1)S(1)} %load.1.cache_ref), custom_call_target="tpu_custom_call" | custom-call | flops 67108864 | bytes 4194304 | tf_op jit(solution)/shard_map/own/pallas_call | solution.py:605
  56.8 3.8 %collective-permute-done.3.got_ref = bf16[1056,128]{1,0:T(8,128)(2,1)S(1)} collective-permute-done((bf16[1056,128]{1,0:T(8,128)(2,1)S(1)}, bf16[1056,128]{1,0:T(8,128)(2,1)S(1)}, u32[]{:S(2)}, u32[]{:S(2)}) %collective-permute-start.3) | collective-permute-done | bytes 270368 | tf_op jit(solution)/shard_map/ppermute | solution.py:22
  60.6 1.3 %merge.1 = bf16[128,1024]{1,0:T(8,128)(2,1)} custom-call(f32[1024,128]{1,0:T(8,128)S(1)} %get-tuple-element.31.own_ref, f32[1024,1]{1,0:T(8,128)S(1)} %get-tuple-element.32.level_ref, bf16[1056,128]{1,0:T(8,128)(2,1)S(1)} %collective-permute-done.3.got_ref), custom_call_target="tpu_custom_call" | custom-call | tf_op jit(solution)/shard_map/merge/pallas_call | solution.py:618
Async XLA Ops:
  0.0 5.8 %collective-permute-start = (bf16[128,8192]{1,0:T(8,128)(2,1)}, bf16[128,8192]{1,0:T(8,128)(2,1)S(1)}, u32[]{:S(2)}, u32[]{:S(2)}) collective-permute-start(bf16[128,8192]{1,0:T(8,128)(2,1)} %bitcast.15), channel_id=1, source_target_pairs={{0,1},{1,0},{2,3},{3,2},{4,5},{5,4},{6,7},{7,6},{8,9},{9,8},{10,11... | collective-permute-start | bytes 6291464 | tf_op jit(solution)/shard_map/ppermute | solution.py:22
  0.5 5.4 %collective-permute-start.1 = (s32[1,64]{1,0:T(1,128)}, s32[1,64]{1,0:T(1,128)S(1)}, u32[]{:S(2)}, u32[]{:S(2)}) collective-permute-start(s32[1,64]{1,0:T(1,128)} %bitcast.18), channel_id=1, source_target_pairs={{0,1},{1,0},{2,3},{3,2},{4,5},{5,4},{6,7},{7,6},{8,9},{9,8},{10,11... | collective-permute-start | bytes 776 | tf_op jit(solution)/shard_map/ppermute | solution.py:22
  5.9 20.2 %copy-start = (s32[64]{0:T(128)S(1)}, s32[64]{0:T(128)}, u32[]{:S(2)}) copy-start(s32[64]{0:T(128)} %lengths_ref.3) | copy-start | bytes 772
  5.9 20.2 %copy-start.1 = (f32[1,128]{1,0:T(1,128)S(1)}, f32[1,128]{1,0:T(1,128)}, u32[]{:S(2)}) copy-start(f32[1,128]{1,0:T(1,128)} %constant.2.clone.freq_ref) | copy-start | bytes 1540
  18.7 21.9 %all-to-all-start = ((bf16[16,16,1024]{2,1,0:T(8,128)(2,1)}), bf16[16,16,1024]{2,1,0:T(8,128)(2,1)S(1)}, u32[]{:S(2)}, u32[]{:S(2)}) async-start(bf16[16,16,1024]{2,1,0:T(8,128)(2,1)} %lora.1), calls=%async_computation | async-start | bytes 1048576 | tf_op jit(solution)/shard_map/all_to_all | solution.py:513
  41.0 9.0 %collective-permute-start.2 = (bf16[1152,128]{1,0:T(8,128)(2,1)S(1)}, bf16[1152,128]{1,0:T(8,128)(2,1)S(1)}, u32[]{:S(2)}, u32[]{:S(2)}) collective-permute-start(bf16[1152,128]{1,0:T(8,128)(2,1)S(1)} %query.1.after.sent_ref), channel_id=1, source_target_pairs={{0,2},{2,0},{4,6},{6,4},{8,10},{10,8},{12,14},{14,12},{1,3},{3,1},... | collective-permute-start | bytes 884744 | tf_op jit(solution)/shard_map/ppermute | solution.py:22
  52.8 7.8 %collective-permute-start.3 = (bf16[1056,128]{1,0:T(8,128)(2,1)S(1)}, bf16[1056,128]{1,0:T(8,128)(2,1)S(1)}, u32[]{:S(2)}, u32[]{:S(2)}) collective-permute-start(bf16[1056,128]{1,0:T(8,128)(2,1)S(1)} %send.1), channel_id=1, source_target_pairs={{0,2},{2,0},{4,6},{6,4},{8,10},{10,8},{12,14},{14,12},{1,3},{3,1},... | collective-permute-start | bytes 811016 | tf_op jit(solution)/shard_map/ppermute | solution.py:22

commit v2 on v1

--- a/solution.py
+++ b/solution.py
@@ -55,18 +55,64 @@
     return owner, local_row, place
 
 
-def stage_kernel(states_hbm, down_hbm, adapters_hbm, table_hbm, *rest):
-    states, down, adapters, table, sem, other_sem = rest
+def picked(dims, pools, states_ref, adapters, table):
+    steps, requests, capacity, per_owner, pool_count = dims
+    owner, local_row, place = routes(adapters, table, per_owner)
+    owner = jnp.concatenate([owner] * steps, axis=1)
+    place = jnp.concatenate([place] * steps, axis=1)
+    local_row = jnp.concatenate([local_row] * steps, axis=1)
+    shape = (steps * capacity, steps * requests)
+    row = iota(shape, 0)
+    row_step = row // capacity
+    slot = (place == row - row_step * capacity) & (row_step == iota(shape, 1) // requests)
+    hits = [
+        slot & (owner == lax.axis_index("tensor") * pool_count + pool) for pool in pools
+    ]
+    pick = jnp.concatenate([jnp.where(hit, 1.0, 0.0) for hit in hits], axis=0).astype(BF)
+    states = jnp.dot(pick, states_ref[...], preferred_element_type=F32).astype(BF)
+    rows = [jnp.sum(jnp.where(hit, local_row, 0), axis=1, keepdims=True) for hit in hits]
+    return states, rows
+
+
+def stage_kernel(dims, states_hbm, down_hbm, adapters_hbm, table_hbm, *rest):
+    states, down, adapters, table, own, own_rows, other, other_rows, sem, other_sem = rest
+    parts = sem.shape[0]
+    size = down.shape[0] // parts
+    first = [
+        pltpu.make_async_copy(adapters_hbm, adapters, other_sem.at[1]),
+        pltpu.make_async_copy(table_hbm, table, other_sem.at[2]),
+        pltpu.make_async_copy(states_hbm, states, other_sem.at[0]),
+    ]
+    copies = []
+    for part in range(parts):
+        span = pl.ds(part * size, size)
+        copies.append(pltpu.make_async_copy(down_hbm.at[span], down.at[span], sem.at[part]))
+    for copy in first + copies:
+        copy.start()
+    for copy in first:
+        copy.wait()
+    pool = lax.axis_index("pool")
+    chosen, rows = picked(dims, (pool, 1 - pool), states, adapters[...], table[...])
+    count = own.shape[0]
+    own[...] = chosen[:count]
+    other[...] = chosen[count:]
+    own_rows[...] = rows[0]
+    other_rows[...] = rows[1]
+    for copy in copies:
+        copy.wait()
+
+
+def more_kernel(first_row, down_hbm, after, down, sem):
     parts = sem.shape[0]
     size = down.shape[0] // parts
     copies = [
-        pltpu.make_async_copy(states_hbm, states, other_sem.at[0]),
-        pltpu.make_async_copy(adapters_hbm, adapters, other_sem.at[1]),
-        pltpu.make_async_copy(table_hbm, table, other_sem.at[2]),
+        pltpu.make_async_copy(
+            down_hbm.at[pl.ds(first_row + part * size, size)],
+            down.at[pl.ds(part * size, size)],
+            sem.at[part],
+        )
+        for part in range(parts)
     ]
-    for part in range(parts):
-        span = pl.ds(part * size, size)
-        copies.append(pltpu.make_async_copy(down_hbm.at[span], down.at[span], sem.at[part]))
     for copy in copies:
         copy.start()
     for copy in copies:
@@ -75,24 +121,25 @@
 
 def lora_kernel(
     dims,
+    rank,
     own_ref,
+    own_rows_ref,
     other_ref,
-    own_adapters_ref,
-    other_adapters_ref,
-    table_ref,
-    down,
+    other_rows_ref,
+    down_first,
+    down_second,
     down_hbm,
     up_hbm,
     out_ref,
     down_rest,
     up,
-    chosen,
     low,
     down_sem,
     up_sem,
 ):
-    steps, requests, capacity, per_owner, rank, tensor_count, pool_count = dims
-    here_rows = down.shape[0]
+    steps, requests, capacity, per_owner, pool_count = dims
+    rows = steps * capacity
+    here_rows = down_first.shape[0] + down_second.shape[0]
     down_rows = down_rest.shape[0]
     up_parts = up_sem.shape[0]
     up_columns = up.shape[1] // up_parts
@@ -113,57 +160,35 @@
         up_copy(part).start()
 
     pool = lax.axis_index("pool")
-    me = lax.axis_index("tensor") * pool_count + pool
-    table = table_ref[...]
-    rows = steps * capacity
-    local_rows = []
-    for which, (states_ref, adapters_ref) in enumerate(
-        ((own_ref, own_adapters_ref), (other_ref, other_adapters_ref))
-    ):
-        owner, local_row, place = routes(adapters_ref[...], table, per_owner)
-        owner = jnp.concatenate([owner] * steps, axis=1)
-        place = jnp.concatenate([place] * steps, axis=1)
-        local_row = jnp.concatenate([local_row] * steps, axis=1)
-        shape = (rows, steps * requests)
-        row = iota(shape, 0)
-        row_step = row // capacity
-        hit = (
-            (owner == me)
-            & (place == row - row_step * capacity)
-            & (row_step == iota(shape, 1) // requests)
-        )
-        local_rows.append(jnp.sum(jnp.where(hit, local_row, 0), axis=1, keepdims=True))
-        pick = jnp.where(hit, 1.0, 0.0).astype(BF)
-        chosen[which] = jnp.dot(
-            pick, states_ref[...], preferred_element_type=F32
-        ).astype(BF)
-    local_rows = jnp.concatenate(local_rows, axis=0)
-    states = jnp.concatenate([chosen[0], chosen[1]], axis=0)
+    local_rows = jnp.concatenate([own_rows_ref[...], other_rows_ref[...]], axis=0)
+    states = jnp.concatenate([own_ref[...].astype(F32), other_ref[...].astype(F32)], axis=0).T.astype(BF)
 
     def factors_of(rows_ref, first_row):
         count = rows_ref.shape[0]
         piece = lax.dot_general(
-            rows_ref[...], states, (((1,), (1,)), ((), ())), preferred_element_type=F32
+            rows_ref[...], states, (((1,), (0,)), ((), ())), preferred_element_type=F32
         ).T
         holder = (iota(piece.shape, 1) + first_row) // rank
         low[:, pl.ds(first_row, count)] = jnp.where(
             holder == local_rows, piece.astype(BF), jnp.zeros(piece.shape, BF)
         )
 
-    for first_row in range(0, here_rows, down_rows):
-        factors_of(down.at[pl.ds(first_row, down_rows)], first_row)
+    first_row = 0
+    for staged in (down_first, down_second):
+        for at in range(0, staged.shape[0], down_rows):
+            factors_of(staged.at[pl.ds(at, down_rows)], first_row)
+            first_row += down_rows
 
     @pl.loop(0, 1)
     def _(_):
         rest_copy.wait()
 
     factors_of(down_rest, here_rows)
-
-    @pl.loop(0, up_parts)
-    def _(part):
+    factors = low[...]
+    for part in range(up_parts):
         up_copy(part).wait()
-        columns = pl.ds(pl.multiple_of(part * up_columns, up_columns), up_columns)
-        term = jnp.dot(low[...], up[:, columns], preferred_element_type=F32).astype(BF)
+        columns = pl.ds(part * up_columns, up_columns)
+        term = jnp.dot(factors, up[:, columns], preferred_element_type=F32).astype(BF)
         out_ref[part * pool_count + pool] = term[:rows]
         out_ref[part * pool_count + 1 - pool] = term[rows:]
 
@@ -251,7 +276,7 @@
 
 
 def query_kernel(
-    dims, terms_ref, spread_ref, projected_ref, piece_ref, cosine_ref, sine_ref, out_ref, packed
+    dims, terms_ref, spread_ref, projected_ref, piece_ref, cosine_ref, sine_ref, first_ref, second_ref, packed
 ):
     steps, requests, heads, head_width = dims
     correction = jnp.dot(spread_ref[...], terms_ref[...], preferred_element_type=F32)
@@ -266,30 +291,33 @@
             packed[pl.ds(step * heads + head, requests, stride=steps * heads), :] = vector[
                 step * requests : (step + 1) * requests
             ]
-    out_ref[:count, :] = packed[...].astype(BF)
-    out_ref[count:, :] = piece_ref[...]
-
-
-def attend(dims, lengths_ref, query_ref, cache_ref, keys, vals, scratch, store):
+    half = count // 2
+    first_ref[:half, :] = packed[:half, :].astype(BF)
+    first_ref[half:, :] = piece_ref[...]
+    second_ref[...] = packed[half:, :].astype(BF)
+
+
+def attend(dims, first_request, lengths_ref, query_ref, cache_ref, keys, vals, scratch, store):
     steps, requests, heads, head_width, kv_split = dims
     scores_ref, recent_ref, weights_ref, new_weights_ref, acc_ref = scratch
     per_request = steps * heads
-    count = requests * per_request
+    mine = requests // 2
+    count = mine * per_request
     scale = head_width ** (-0.5)
     context = cache_ref.shape[2]
     part = lax.axis_index("tensor") % kv_split
     base = part * context
     lane = iota((per_request, context), 1)
-    for request in range(requests):
+    for request in range(mine):
         span = pl.ds(request * per_request, per_request)
         score = lax.dot_general(
             query_ref[span, :],
-            cache_ref[request, 0],
+            cache_ref[first_request + request, 0],
             (((1,), (1,)), ((), ())),
             preferred_element_type=F32,
         )
         scores_ref[span, :] = jnp.where(
-            lane < lengths_ref[request] - base, score * scale, MASKED
+            lane < lengths_ref[first_request + request] - base, score * scale, MASKED
         )
     rows = min(128, count)
     shape = (rows, steps * requests)
@@ -305,7 +333,7 @@
             query_ref[span, :], keys, (((1,), (1,)), ((), ())), preferred_element_type=F32
         )
         recent_ref[span, :] = jnp.where(
-            allowed & (ahead == at * (rows // per_request)), recent * scale, MASKED
+            allowed & (ahead == first_request + at * (rows // per_request)), recent * scale, MASKED
         )
     totals = []
     for at in range(count // rows):
@@ -327,10 +355,12 @@
         weights_ref[span, :] = e_cached.astype(BF)
         new_weights_ref[span, :] = e_recent.astype(BF)
         totals.append((top, total))
-    for request in range(requests):
+    for request in range(mine):
         span = pl.ds(request * per_request, per_request)
         acc_ref[span, :] = jnp.dot(
-            weights_ref[span, :], cache_ref[request, 1], preferred_element_type=F32
+            weights_ref[span, :],
+            cache_ref[first_request + request, 1],
+            preferred_element_type=F32,
         )
     for at in range(count // rows):
         span = pl.ds(at * rows, rows)
@@ -348,7 +378,9 @@
     return keys, vals
 
 
-def own_kernel(dims, lengths_ref, sent_ref, got_ref, cache_ref, out_ref, level_ref, *scratch):
+def own_kernel(
+    dims, first, lengths_ref, sent_ref, got_ref, query_ref, cache_ref, out_ref, level_ref, *scratch
+):
     count = out_ref.shape[0]
     keys, vals = new_pieces(sent_ref[count:, :], got_ref[count:, :])
 
@@ -356,10 +388,12 @@
         out_ref[pl.ds(at * rows, rows), :] = result
         level_ref[pl.ds(at * rows, rows), :] = level
 
-    attend(dims, lengths_ref, sent_ref, cache_ref, keys, vals, scratch, store)
-
-
-def send_kernel(dims, lengths_ref, sent_ref, got_ref, cache_ref, out_ref, levels, *scratch):
+    attend(dims, first, lengths_ref, query_ref, cache_ref, keys, vals, scratch, store)
+
+
+def send_kernel(
+    dims, first, lengths_ref, sent_ref, got_ref, query_ref, cache_ref, out_ref, levels, *scratch
+):
     lines = levels.shape[0]
     count = lines * 128
     keys, vals = new_pieces(sent_ref[count:, :], got_ref[count:, :])
@@ -371,7 +405,7 @@
                 level[line * 128 : (line + 1) * 128]
             )
 
-    attend(dims, lengths_ref, got_ref, cache_ref, keys, vals, scratch, store)
+    attend(dims, first, lengths_ref, query_ref, cache_ref, keys, vals, scratch, store)
     rest = levels[...]
     pieces = []
     for _ in range(3):
@@ -382,23 +416,26 @@
     out_ref[pl.ds(count, 4 * lines), :] = jnp.concatenate(pieces, axis=0)
 
 
-def merge_kernel(dims, own_ref, level_ref, got_ref, out_ref, packed):
+def merge_kernel(dims, *refs):
     steps, requests, heads, head_width = dims
-    count = own_ref.shape[0]
-    lines = count // 128
-    extra = got_ref[pl.ds(count, 4 * lines), :].astype(F32)
-    other_level = extra[:lines] + extra[lines : 2 * lines] + extra[2 * lines : 3 * lines]
-    for line in range(lines):
-        span = pl.ds(line * 128, 128)
-        theirs = column_of(other_level[line : line + 1])
-        mine = level_ref[span, :]
-        top = jnp.maximum(mine, theirs)
-        mine = jnp.exp(mine - top)
-        theirs = jnp.exp(theirs - top)
-        total = mine + theirs
-        packed[span, :] = own_ref[span, :] * (mine / total) + got_ref[span, :].astype(F32) * (
-            theirs / total
-        )
+    out_ref, packed = refs[6:]
+    for half in range(2):
+        own_ref, level_ref, got_ref = refs[3 * half : 3 * half + 3]
+        count = own_ref.shape[0]
+        lines = count // 128
+        extra = got_ref[pl.ds(count, 4 * lines), :].astype(F32)
+        other_level = extra[:lines] + extra[lines : 2 * lines] + extra[2 * lines : 3 * lines]
+        for line in range(lines):
+            span = pl.ds(line * 128, 128)
+            theirs = column_of(other_level[line : line + 1])
+            mine = level_ref[span, :]
+            top = jnp.maximum(mine, theirs)
+            mine = jnp.exp(mine - top)
+            theirs = jnp.exp(theirs - top)
+            total = mine + theirs
+            packed[pl.ds(half * count + line * 128, 128), :] = own_ref[span, :] * (
+                mine / total
+            ) + got_ref[span, :].astype(F32) * (theirs / total)
     for step in range(steps):
         for head in range(heads):
             out_ref[
@@ -450,8 +487,6 @@
 
     flat = inputs.reshape(count, width)
     adapters = request_adapter.reshape(1, requests)
-    other_adapters = swapped(adapters, "pool", 0)
-    other_flat = swapped(flat, "pool", 0)
     table = adapter_storage_row.reshape(1, -1)
     down = adapter_down_factors.reshape(per_owner * rank, width)
     up = adapter_up_factors.reshape(per_owner * rank, -1)
@@ -459,41 +494,53 @@
     anywhere = pl.BlockSpec(memory_space=pltpu.HBM)
     smem = pl.BlockSpec(memory_space=pltpu.SMEM)
 
-    rest_rows = per_owner * rank // 4
-    here_rows = per_owner * rank - rest_rows
-    flat_here, down_here, adapters, table = pl.pallas_call(
-        stage_kernel,
+    quarter = per_owner * rank // 4
+    lora_dims = (steps, requests, capacity, per_owner, pool_count)
+    flat_here, down_first, adapters, table, own, own_rows, others, others_rows = pl.pallas_call(
+        functools.partial(stage_kernel, lora_dims),
         out_shape=[
             in_vmem(flat.shape, BF),
-            in_vmem((here_rows, width), BF),
+            in_vmem((quarter, width), BF),
             in_vmem(adapters.shape, I32),
             in_vmem(table.shape, I32),
+            in_vmem((rows, width), BF),
+            in_vmem((rows, 1), I32),
+            in_vmem((rows, width), BF),
+            in_vmem((rows, 1), I32),
         ],
         in_specs=[anywhere] * 4,
-        out_specs=whole(*range(4)),
-        scratch_shapes=[pltpu.SemaphoreType.DMA((3,)), pltpu.SemaphoreType.DMA((3,))],
-        compiler_params=vmem_limit(4),
-        cost_estimate=pl.CostEstimate(
-            flops=0, bytes_accessed=2 * (down.size + flat.size), transcendentals=0
-        ),
+        out_specs=whole(*range(8)),
+        scratch_shapes=[pltpu.SemaphoreType.DMA((2,)), pltpu.SemaphoreType.DMA((3,))],
+        compiler_params=vmem_limit(8),
         name="stage",
     )(in_hbm(flat), in_hbm(down), in_hbm(adapters), in_hbm(table))
-
-    lora_dims = (steps, requests, capacity, per_owner, rank, tensor_count, pool_count)
+    others = swapped(others, "pool", 0)
+    others_rows = swapped(others_rows, "pool", 0)
+
+    down_second = pl.pallas_call(
+        functools.partial(more_kernel, quarter),
+        out_shape=in_vmem((2 * quarter, width), BF),
+        in_specs=[anywhere, pl.BlockSpec(memory_space=pl.ANY)],
+        out_specs=whole(0)[0],
+        scratch_shapes=[pltpu.SemaphoreType.DMA((4,))],
+        compiler_params=vmem_limit(1),
+        cost_estimate=pl.CostEstimate(flops=0, bytes_accessed=2 * down.size, transcendentals=0),
+        name="more",
+    )(in_hbm(down), own_rows)
+
     outgoing = pl.pallas_call(
-        functools.partial(lora_kernel, lora_dims),
+        functools.partial(lora_kernel, lora_dims, rank),
         out_shape=jax.ShapeDtypeStruct((owners, rows, query_columns), BF),
         in_specs=whole(*range(6)) + [anywhere] * 2,
         out_specs=whole(0)[0],
         scratch_shapes=[
-            pltpu.VMEM((rest_rows, width), BF),
+            pltpu.VMEM((quarter, width), BF),
             pltpu.VMEM(up.shape, BF),
-            pltpu.VMEM((2, rows, width), BF),
             pltpu.VMEM((2 * rows, per_owner * rank), BF),
             pltpu.SemaphoreType.DMA((1,)),
             pltpu.SemaphoreType.DMA((tensor_count,)),
         ],
-        compiler_params=vmem_limit(24),
+        compiler_params=vmem_limit(28),
         cost_estimate=pl.CostEstimate(
             flops=8 * rows * per_owner * rank * width,
             bytes_accessed=2 * per_owner * rank * width,
@@ -501,12 +548,12 @@
         ),
         name="lora",
     )(
-        flat_here,
-        pltpu.with_memory_space_constraint(other_flat, pltpu.VMEM),
-        adapters,
-        other_adapters,
-        table,
-        down_here,
+        own,
+        own_rows,
+        pltpu.with_memory_space_constraint(others, pltpu.VMEM),
+        pltpu.with_memory_space_constraint(others_rows, pltpu.VMEM),
+        down_first,
+        down_second,
         in_hbm(down),
         in_hbm(up),
     )
@@ -534,7 +581,7 @@
             pltpu.VMEM(key_value_weight.shape, BF),
             pltpu.SemaphoreType.DMA((17,)),
         ],
-        compiler_params=vmem_limit(24),
+        compiler_params=vmem_limit(28),
         cost_estimate=pl.CostEstimate(
             flops=2 * count * width * query_columns,
             bytes_accessed=2 * width * query_columns,
@@ -553,16 +600,21 @@
 
     dims = (steps, requests, heads, head_width)
     packed_rows = count * heads
-    sent = pl.pallas_call(
+    half_rows = packed_rows // 2
+    sent, sent_second = pl.pallas_call(
         functools.partial(query_kernel, dims),
-        out_shape=jax.ShapeDtypeStruct((packed_rows + count, head_width), BF),
+        out_shape=[
+            jax.ShapeDtypeStruct((half_rows + count, head_width), BF),
+            jax.ShapeDtypeStruct((half_rows, head_width), BF),
+        ],
         in_specs=whole(*range(6)),
-        out_specs=whole(0)[0],
+        out_specs=whole(*range(2)),
         scratch_shapes=[pltpu.VMEM((packed_rows, head_width), F32)],
         compiler_params=vmem_limit(8),
         name="query",
     )(terms, spread, projected, own_piece, cosine, sine)
     got = swapped(sent, "tensor", 0)
+    got_second = swapped(sent_second, "tensor", 0)
 
     cache_here = pl.pallas_call(
         load_kernel,
@@ -577,53 +629,60 @@
         name="load",
     )(in_hbm(cache), sent)
 
-    lines = packed_rows // 128
+    lines = half_rows // 128
     attend_dims = (steps, requests, heads, head_width, kv_split)
     attend_scratch = [
-        pltpu.VMEM((packed_rows, context), F32),
-        pltpu.VMEM((packed_rows, count), F32),
-        pltpu.VMEM((packed_rows, context), BF),
-        pltpu.VMEM((packed_rows, count), BF),
-        pltpu.VMEM((packed_rows, head_width), F32),
+        pltpu.VMEM((half_rows, context), F32),
+        pltpu.VMEM((half_rows, count), F32),
+        pltpu.VMEM((half_rows, context), BF),
+        pltpu.VMEM((half_rows, count), BF),
+        pltpu.VMEM((half_rows, head_width), F32),
     ]
     cost = pl.CostEstimate(
-        flops=4 * packed_rows * context * head_width,
-        bytes_accessed=2 * cache.size,
-        transcendentals=packed_rows * context,
-    )
-    sending = pl.pallas_call(
-        functools.partial(send_kernel, attend_dims),
-        out_shape=jax.ShapeDtypeStruct((packed_rows + 4 * lines, head_width), BF),
-        in_specs=[smem] + whole(*range(3)),
-        out_specs=whole(0)[0],
-        scratch_shapes=[pltpu.VMEM((lines, 128), F32)] + attend_scratch,
-        compiler_params=vmem_limit(12),
-        cost_estimate=cost,
-        name="send",
-    )(lengths, sent, got, cache_here)
-    partial = swapped(sending, "tensor", 0)
-    own, level = pl.pallas_call(
-        functools.partial(own_kernel, attend_dims),
-        out_shape=[
-            jax.ShapeDtypeStruct((packed_rows, head_width), F32),
-            jax.ShapeDtypeStruct((packed_rows, 1), F32),
-        ],
-        in_specs=[smem] + whole(*range(3)),
-        out_specs=whole(*range(2)),
-        scratch_shapes=attend_scratch,
-        compiler_params=vmem_limit(12),
-        cost_estimate=cost,
-        name="own",
-    )(lengths, sent, got, cache_here)
+        flops=2 * packed_rows * context * head_width,
+        bytes_accessed=cache.size,
+        transcendentals=half_rows * context,
+    )
+    partials = []
+    sending = None
+    for half, other_query in enumerate((got, got_second)):
+        sending = pl.pallas_call(
+            functools.partial(send_kernel, attend_dims, half * (requests // 2)),
+            out_shape=jax.ShapeDtypeStruct((half_rows + 4 * lines, head_width), BF),
+            in_specs=[smem] + whole(*range(4)),
+            out_specs=whole(0)[0],
+            scratch_shapes=[pltpu.VMEM((lines, 128), F32)] + attend_scratch,
+            compiler_params=vmem_limit(16),
+            cost_estimate=cost,
+            name="send",
+        )(lengths, sent, got, other_query, cache_here)
+        partials.append(swapped(sending, "tensor", 0))
+    queries = lax.optimization_barrier((sent, sent_second, sending))
+    merging = []
+    for half in range(2):
+        own, level = pl.pallas_call(
+            functools.partial(own_kernel, attend_dims, half * (requests // 2)),
+            out_shape=[
+                jax.ShapeDtypeStruct((half_rows, head_width), F32),
+                jax.ShapeDtypeStruct((half_rows, 1), F32),
+            ],
+            in_specs=[smem] + whole(*range(4)),
+            out_specs=whole(*range(2)),
+            scratch_shapes=attend_scratch,
+            compiler_params=vmem_limit(16),
+            cost_estimate=cost,
+            name="own",
+        )(lengths, sent, got, queries[half], cache_here)
+        merging += [own, level, partials[half]]
     attended = pl.pallas_call(
         functools.partial(merge_kernel, dims),
         out_shape=jax.ShapeDtypeStruct((count, query_columns), BF),
-        in_specs=whole(*range(3)),
+        in_specs=whole(*range(6)),
         out_specs=whole(0)[0],
         scratch_shapes=[pltpu.VMEM((packed_rows, head_width), F32)],
         compiler_params=vmem_limit(8),
         name="merge",
-    )(own, level, partial)
+    )(*merging)
     return attended.reshape(steps, requests, query_columns)
 
 

time: 62.2 us -> 57.7 us (0.928)
  waiting for transfers between devices: 17 us -> 10.1 us
  starting transfers between devices: 9.59 us -> 12.2 us
    ppermute x4 -> x6, waiting for transfers between devices: 10.1 us -> 3.25 us  [swapped(): return lax.ppermute(value, axis, pairs)]
    ppermute x4 -> x6, starting transfers between devices: 2.19 us -> 4.84 us  [swapped(): return lax.ppermute(value, axis, pairs)]
    pallas_call x5 -> x8, Pallas kernels: 24.1 us -> 23.8 us  [the longest x1 9.63 us: local(): pl.pallas_call(functools.partial(lora_kernel, lora_dims, rank), out_shape...]
  transfers between devices with their start and end apart: 5 -> 7, of which waited for: 3 -> 3; matrix products, arithmetic and copies ran while one was open for 0% -> 0% of each run, Pallas kernels for 29% -> 29%
where the time goes in v2:
time: 57.7 us; the launch traced here: 57.4 us
  Pallas kernels  34.9 us (60%)
  starting transfers between devices  12.2 us (21%)
  waiting for transfers between devices  10.1 us (18%)
    pallas_call x1, Pallas kernels, local(): pl.pallas_call(functools.partial(lora_kernel, lora_dims, rank), out_shape...  9.63 us
    pallas_call x1, Pallas kernels, local(): pl.pallas_call(functools.partial(project_kernel, (steps, requests, capaci...  7.55 us
    all_to_all x1, starting transfers between devices, local(): lax.all_to_all(outgoing, ('tensor', 'pool'), split_axis=0, concat_axis=0,...  7.38 us
    all_to_all x1, waiting for transfers between devices, local(): lax.all_to_all(outgoing, ('tensor', 'pool'), split_axis=0, concat_axis=0,...  6.88 us
    ppermute x6, starting transfers between devices, swapped(): return lax.ppermute(value, axis, pairs)  4.84 us
    pallas_call x2, Pallas kernels, local(): pl.pallas_call(functools.partial(send_kernel, attend_dims, half * (reques...  3.59 us
    pallas_call x2, Pallas kernels, local(): pl.pallas_call(functools.partial(own_kernel, attend_dims, half * (request...  3.58 us
    pallas_call x1, Pallas kernels, local(): pl.pallas_call(functools.partial(more_kernel, quarter), out_shape=in_vmem...  3.5 us
  transfers between devices with their start and end apart: 7, of which 3 were waited for; matrix products, arithmetic and copies ran while one was open for 0% of the time, Pallas kernels for 29%

profile of v2, /device:TPU:0, one launch (start us, length us, event | category | flops | bytes accessed | tf_op | source)
XLA Modules:
  0.0 57.4 jit_solution(11799290304109449752)
XLA Ops:
  0.0 3.1 %stage.1 = (bf16[128,8192]{1,0:T(8,128)(2,1)S(1)}, bf16[256,8192]{1,0:T(8,128)(2,1)S(1)}, s32[1,64]{1,0:T(1,128)S(1)}, s32[1,256]{1,0:T(1,128)S(1)}, bf16[16,819...) custom-call(bf16[128,8192]{1,0:T(8,128)(2,1)} %bitcast.16, ...), custom_call_target="tpu_custom_call" | custom-call | tf_op jit(solution)/shard_map/stage/pallas_call | solution.py:499
  3.1 0.5 collective-permute-start
  3.6 0.1 collective-permute-start.1
  3.7 3.5 %more.1.down_second = bf16[512,8192]{1,0:T(8,128)(2,1)S(1)} custom-call(bf16[1024,8192]{1,0:T(8,128)(2,1)} %bitcast.12, s32[16,1]{1,0:T(8,128)S(1)} %get-tuple-element.30.after.own_rows_ref), custom_call_target="tpu_custom_call" | custom-call | bytes 16777216 | tf_op jit(solution)/shard_map/more/pallas_call | solution.py:520
  7.2 0.0 collective-permute-done.1.other_rows_ref
  7.2 0.0 copy-start
  7.2 0.0 copy-start.1
  7.2 9.6 %lora.1 = bf16[16,16,1024]{2,1,0:T(8,128)(2,1)} custom-call(bf16[16,8192]{1,0:T(8,128)(2,1)S(1)} %get-tuple-element.29.own_ref, s32[16,1]{1,0:T(8,128)S(1)} %get-tuple-element.30.after.own_rows_ref, bf16[16,8192]{1,0:T(8,128)(2,1)S(1)} %collective-permute-done.other_ref, s32[16,1]{1,0:T(8,128)S(1)} %collective-permute-done.1.other_rows_ref, ...), custom_call_target="tpu_custom_call" | custom-call | flops 1073741824 | bytes 16777216 | tf_op jit(solution)/shard_map/lora/pallas_call | solution.py:531
  16.9 7.4 %all-to-all-start = ((bf16[16,16,1024]{2,1,0:T(8,128)(2,1)}), bf16[16,16,1024]{2,1,0:T(8,128)(2,1)S(1)}, u32[]{:S(2)}, u32[]{:S(2)}) async-start(bf16[16,16,1024]{2,1,0:T(8,128)(2,1)} %lora.1), calls=%async_computation | async-start | bytes 1048576 | tf_op jit(solution)/shard_map/all_to_all | solution.py:560
  24.3 7.5 %project.1 = (f32[128,1024]{1,0:T(8,128)S(1)}, bf16[128,128]{1,0:T(8,128)(2,1)S(1)}, f32[128,128]{1,0:T(8,128)S(1)}, f32[128,128]{1,0:T(8,128)S(1)}, bf16[128,256]{1,0:T(8,128)(2,1)S(1)}) custom-call(bf16[128,8192]{1,0:T(8,128)(2,1)S(1)} %get-tuple-element.37.states_ref, s32[1,64]{1,0:T(1,128)S(1)} %get-tuple-element.38.adapters_ref, ...), custom_call_target="tpu_custom_call" | custom-call | flops 2147483648 | bytes 16777216 | tf_op jit(solution)/shard_map/project/pallas_call | solution.py:568
  31.8 6.9 %all-to-all-done = bf16[16,16,1024]{2,1,0:T(8,128)(2,1)S(1)} async-done(((bf16[16,16,1024]{2,1,0:T(8,128)(2,1)}), bf16[16,16,1024]{2,1,0:T(8,128)(2,1)S(1)}, u32[]{:S(2)}, u32[]{:S(2)}) %all-to-all-start) | async-done | bytes 524320 | tf_op jit(solution)/shard_map/all_to_all | solution.py:560
  38.7 0.5 query.1
  39.2 0.5 collective-permute-start.2
  39.6 1.6 %collective-permute-start.3 = (bf16[512,128]{1,0:T(8,128)(2,1)S(1)}, bf16[512,128]{1,0:T(8,128)(2,1)S(1)}, u32[]{:S(2)}, u32[]{:S(2)}) collective-permute-start(bf16[512,128]{1,0:T(8,128)(2,1)S(1)} %get-tuple-element.50.query_ref), channel_id=1, source_target_pairs={{0,2},{2,0},{4,6},{6,4},{8,10},{10,8},{12,14},{14,12},{1,3},{3,1},... | collective-permute-start | bytes 393224 | tf_op jit(solution)/shard_map/ppermute | solution.py:22
  41.3 2.2 %load.1.cache_ref = bf16[64,2,128,128]{3,2,1,0:T(8,128)(2,1)S(1)} custom-call(bf16[64,2,128,128]{3,2,1,0:T(8,128)(2,1)} %bitcast.15, bf16[640,128]{1,0:T(8,128)(2,1)S(1)} %get-tuple-element.47.after.sent_ref.query_ref), custom_call_target="tpu_custom_call" | custom-call | bytes 8388608 | tf_op jit(solution)/shard_map/load/pallas_call | solution.py:619
  43.5 2.8 %collective-permute-done.2.got_ref.query_ref = bf16[640,128]{1,0:T(8,128)(2,1)S(1)} collective-permute-done((bf16[640,128]{1,0:T(8,128)(2,1)S(1)}, bf16[640,128]{1,0:T(8,128)(2,1)S(1)}, u32[]{:S(2)}, u32[]{:S(2)}) %collective-permute-start.2) | collective-permute-done | bytes 163872 | tf_op jit(solution)/shard_map/ppermute | solution.py:22
  46.3 1.8 %send.3 = bf16[528,128]{1,0:T(8,128)(2,1)S(1)} custom-call(s32[64]{0:T(128)S(1)} %copy-done, bf16[640,128]{1,0:T(8,128)(2,1)S(1)} %get-tuple-element.47.after.sent_ref.query_ref, bf16[640,128]{1,0:T(8,128)(2,1)S(1)} %collective-permute-done.2.got_ref.query_ref, bf16[640,128]{1,0:T(8,128)(2,1)S(1)} %collective-permute-done.2.got_ref.query_ref, ...), custom_call_target="tpu_custom_call" | custom-call | flops 33554432 | bytes 2097152 | tf_op jit(solution)/shard_map/send/pallas_call | solution.py:649
  48.1 0.5 collective-permute-start.4
  48.6 1.8 %send.2 = bf16[528,128]{1,0:T(8,128)(2,1)S(1)} custom-call(s32[64]{0:T(128)S(1)} %copy-done, bf16[640,128]{1,0:T(8,128)(2,1)S(1)} %get-tuple-element.47.after.sent_ref.query_ref, bf16[640,128]{1,0:T(8,128)(2,1)S(1)} %collective-permute-done.2.got_ref.query_ref, bf16[512,128]{1,0:T(8,128)(2,1)S(1)} %collective-permute-done.3.query_ref, ...), custom_call_target="tpu_custom_call" | custom-call | flops 33554432 | bytes 2097152 | tf_op jit(solution)/shard_map/send/pallas_call | solution.py:649
  50.4 1.7 %collective-permute-start.5 = (bf16[528,128]{1,0:T(8,128)(2,1)S(1)}, bf16[528,128]{1,0:T(8,128)(2,1)S(1)}, u32[]{:S(2)}, u32[]{:S(2)}) collective-permute-start(bf16[528,128]{1,0:T(8,128)(2,1)S(1)} %send.2), channel_id=1, source_target_pairs={{0,2},{2,0},{4,6},{6,4},{8,10},{10,8},{12,14},{14,12},{1,3},{3,1},... | collective-permute-start | bytes 405512 | tf_op jit(solution)/shard_map/ppermute | solution.py:22
  52.1 1.8 %own.2 = (f32[512,128]{1,0:T(8,128)S(1)}, f32[512,1]{1,0:T(8,128)S(1)}) custom-call(s32[64]{0:T(128)S(1)} %copy-done, bf16[640,128]{1,0:T(8,128)(2,1)S(1)} %get-tuple-element.47.after.sent_ref.query_ref, bf16[640,128]{1,0:T(8,128)(2,1)S(1)} %collective-permute-done.2.got_ref.query_ref, bf16[640,128]{1,0:T(8,128)(2,1)S(1)} %get-tuple-element.47.after.sent_ref.query_ref, ...), custom_call_target="tpu_custom_call" | custom-call | flops 33554432 | bytes 2097152 | tf_op jit(solution)/shard_map/own/pallas_call | solution.py:663
  53.9 1.8 %own.3 = (f32[512,128]{1,0:T(8,128)S(1)}, f32[512,1]{1,0:T(8,128)S(1)}) custom-call(s32[64]{0:T(128)S(1)} %copy-done, bf16[640,128]{1,0:T(8,128)(2,1)S(1)} %get-tuple-element.47.after.sent_ref.query_ref, bf16[640,128]{1,0:T(8,128)(2,1)S(1)} %collective-permute-done.2.got_ref.query_ref, bf16[512,128]{1,0:T(8,128)(2,1)S(1)} %get-tuple-element.50.query_ref, ...), custom_call_target="tpu_custom_call" | custom-call | flops 33554432 | bytes 2097152 | tf_op jit(solution)/shard_map/own/pallas_call | solution.py:663
  55.7 0.4 collective-permute-done.5.refs_5_
  56.1 1.3 %merge.1 = bf16[128,1024]{1,0:T(8,128)(2,1)} custom-call(f32[512,128]{1,0:T(8,128)S(1)} %get-tuple-element.48.refs_0_, f32[512,1]{1,0:T(8,128)S(1)} %get-tuple-element.49.refs_1_, bf16[528,128]{1,0:T(8,128)(2,1)S(1)} %collective-permute-done.4.refs_2_, f32[512,128]{1,0:T(8,128)S(1)} %get-tuple-element.51.refs_3_, f32[512,1]{1,0:T(8,128)S(1)} %get-tuple-element.52.refs_4_, ...), custom_call_target="tpu_custom_call" | custom-call | tf_op jit(solution)/shard_map/merge/pallas_call | solution.py:677
  (5 shorter events, 0.0 us)
Async XLA Ops:
  3.1 4.1 %collective-permute-start = (bf16[16,8192]{1,0:T(8,128)(2,1)S(1)}, bf16[16,8192]{1,0:T(8,128)(2,1)S(1)}, u32[]{:S(2)}, u32[]{:S(2)}) collective-permute-start(bf16[16,8192]{1,0:T(8,128)(2,1)S(1)} %get-tuple-element.31), channel_id=1, source_target_pairs={{0,1},{1,0},{2,3},{3,2},{4,5},{5,4},{6,7},{7,6},{8,9},{9,8},{10,11... | collective-permute-start | bytes 786440 | tf_op jit(solution)/shard_map/ppermute | solution.py:22
  3.6 3.6 %collective-permute-start.1 = (s32[16,1]{1,0:T(8,128)S(1)}, s32[16,1]{1,0:T(8,128)S(1)}, u32[]{:S(2)}, u32[]{:S(2)}) collective-permute-start(s32[16,1]{1,0:T(8,128)S(1)} %get-tuple-element.32), channel_id=1, source_target_pairs={{0,1},{1,0},{2,3},{3,2},{4,5},{5,4},{6,7},{7,6},{8,9},{9,8},{10,11... | collective-permute-start | bytes 200 | tf_op jit(solution)/shard_map/ppermute | solution.py:22
  7.2 17.1 %copy-start = (s32[64]{0:T(128)S(1)}, s32[64]{0:T(128)}, u32[]{:S(2)}) copy-start(s32[64]{0:T(128)} %lengths_ref.7) | copy-start | bytes 772
  7.2 17.1 %copy-start.1 = (f32[1,128]{1,0:T(1,128)S(1)}, f32[1,128]{1,0:T(1,128)}, u32[]{:S(2)}) copy-start(f32[1,128]{1,0:T(1,128)} %constant.2.clone.freq_ref) | copy-start | bytes 1540
  16.9 21.9 %all-to-all-start = ((bf16[16,16,1024]{2,1,0:T(8,128)(2,1)}), bf16[16,16,1024]{2,1,0:T(8,128)(2,1)S(1)}, u32[]{:S(2)}, u32[]{:S(2)}) async-start(bf16[16,16,1024]{2,1,0:T(8,128)(2,1)} %lora.1), calls=%async_computation | async-start | bytes 1048576 | tf_op jit(solution)/shard_map/all_to_all | solution.py:560
  39.2 7.1 %collective-permute-start.2 = (bf16[640,128]{1,0:T(8,128)(2,1)S(1)}, bf16[640,128]{1,0:T(8,128)(2,1)S(1)}, u32[]{:S(2)}, u32[]{:S(2)}) collective-permute-start(bf16[640,128]{1,0:T(8,128)(2,1)S(1)} %get-tuple-element.47.after.sent_ref.query_ref), channel_id=1, source_target_pairs={{0,2},{2,0},{4,6},{6,4},{8,10},{10,8},{12,14},{14,12},{1,3},{3,1},... | collective-permute-start | bytes 491528 | tf_op jit(solution)/shard_map/ppermute | solution.py:22
  39.6 8.9 %collective-permute-start.3 = (bf16[512,128]{1,0:T(8,128)(2,1)S(1)}, bf16[512,128]{1,0:T(8,128)(2,1)S(1)}, u32[]{:S(2)}, u32[]{:S(2)}) collective-permute-start(bf16[512,128]{1,0:T(8,128)(2,1)S(1)} %get-tuple-element.50.query_ref), channel_id=1, source_target_pairs={{0,2},{2,0},{4,6},{6,4},{8,10},{10,8},{12,14},{14,12},{1,3},{3,1},... | collective-permute-start | bytes 393224 | tf_op jit(solution)/shard_map/ppermute | solution.py:22
  48.1 7.6 %collective-permute-start.4 = (bf16[528,128]{1,0:T(8,128)(2,1)S(1)}, bf16[528,128]{1,0:T(8,128)(2,1)S(1)}, u32[]{:S(2)}, u32[]{:S(2)}) collective-permute-start(bf16[528,128]{1,0:T(8,128)(2,1)S(1)} %send.3), channel_id=1, source_target_pairs={{0,2},{2,0},{4,6},{6,4},{8,10},{10,8},{12,14},{14,12},{1,3},{3,1},... | collective-permute-start | bytes 405512 | tf_op jit(solution)/shard_map/ppermute | solution.py:22
  50.4 5.7 %collective-permute-start.5 = (bf16[528,128]{1,0:T(8,128)(2,1)S(1)}, bf16[528,128]{1,0:T(8,128)(2,1)S(1)}, u32[]{:S(2)}, u32[]{:S(2)}) collective-permute-start(bf16[528,128]{1,0:T(8,128)(2,1)S(1)} %send.2), channel_id=1, source_target_pairs={{0,2},{2,0},{4,6},{6,4},{8,10},{10,8},{12,14},{14,12},{1,3},{3,1},... | collective-permute-start | bytes 405512 | tf_op jit(solution)/shard_map/ppermute | solution.py:22

commit v3 on v2

--- a/solution.py
+++ b/solution.py
@@ -386,7 +386,10 @@
 
     def store(at, rows, result, level):
         out_ref[pl.ds(at * rows, rows), :] = result
-        level_ref[pl.ds(at * rows, rows), :] = level
+        for line in range(rows // 128):
+            level_ref[pl.ds(at * (rows // 128) + line, 1), :] = row_of(
+                level[line * 128 : (line + 1) * 128]
+            )
 
     attend(dims, first, lengths_ref, query_ref, cache_ref, keys, vals, scratch, store)
 
@@ -424,18 +427,19 @@
         count = own_ref.shape[0]
         lines = count // 128
         extra = got_ref[pl.ds(count, 4 * lines), :].astype(F32)
-        other_level = extra[:lines] + extra[lines : 2 * lines] + extra[2 * lines : 3 * lines]
+        theirs = extra[:lines] + extra[lines : 2 * lines] + extra[2 * lines : 3 * lines]
+        mine = level_ref[...]
+        top = jnp.maximum(mine, theirs)
+        mine = jnp.exp(mine - top)
+        theirs = jnp.exp(theirs - top)
+        total = mine + theirs
+        mine = mine / total
+        theirs = theirs / total
         for line in range(lines):
             span = pl.ds(line * 128, 128)
-            theirs = column_of(other_level[line : line + 1])
-            mine = level_ref[span, :]
-            top = jnp.maximum(mine, theirs)
-            mine = jnp.exp(mine - top)
-            theirs = jnp.exp(theirs - top)
-            total = mine + theirs
-            packed[pl.ds(half * count + line * 128, 128), :] = own_ref[span, :] * (
-                mine / total
-            ) + got_ref[span, :].astype(F32) * (theirs / total)
+            packed[pl.ds(half * count + line * 128, 128), :] = own_ref[span, :] * column_of(
+                mine[line : line + 1]
+            ) + got_ref[span, :].astype(F32) * column_of(theirs[line : line + 1])
     for step in range(steps):
         for head in range(heads):
             out_ref[
@@ -500,7 +504,7 @@
         functools.partial(stage_kernel, lora_dims),
         out_shape=[
             in_vmem(flat.shape, BF),
-            in_vmem((quarter, width), BF),
+            in_vmem((2 * quarter, width), BF),
             in_vmem(adapters.shape, I32),
             in_vmem(table.shape, I32),
             in_vmem((rows, width), BF),
@@ -518,8 +522,8 @@
     others_rows = swapped(others_rows, "pool", 0)
 
     down_second = pl.pallas_call(
-        functools.partial(more_kernel, quarter),
-        out_shape=in_vmem((2 * quarter, width), BF),
+        functools.partial(more_kernel, 2 * quarter),
+        out_shape=in_vmem((quarter, width), BF),
         in_specs=[anywhere, pl.BlockSpec(memory_space=pl.ANY)],
         out_specs=whole(0)[0],
         scratch_shapes=[pltpu.SemaphoreType.DMA((4,))],
@@ -664,7 +668,7 @@
             functools.partial(own_kernel, attend_dims, half * (requests // 2)),
             out_shape=[
                 jax.ShapeDtypeStruct((half_rows, head_width), F32),
-                jax.ShapeDtypeStruct((half_rows, 1), F32),
+                jax.ShapeDtypeStruct((lines, 128), F32),
             ],
             in_specs=[smem] + whole(*range(4)),
             out_specs=whole(*range(2)),

time: 57.7 us -> 57.2 us (level)
    pallas_call x1, Pallas kernels: 3.5 us -> 2.2 us  [local(): pl.pallas_call(functools.partial(more_kernel, 2 * quarter), out_shape=in_...]
    pallas_call x1, Pallas kernels: 3.07 us -> 4.14 us  [local(): pl.pallas_call(functools.partial(stage_kernel, lora_dims), out_shape=[in_...]
  transfers between devices with their start and end apart: 7 -> 7, of which waited for: 3 -> 3; matrix products, arithmetic and copies ran while one was open for 0% -> 0% of each run, Pallas kernels for 29% -> 27%
where the time goes in v3:
time: 57.2 us; the launch traced here: 57 us
  Pallas kernels  34.5 us (60%)
  starting transfers between devices  12.2 us (21%)
  waiting for transfers between devices  10.1 us (18%)
    pallas_call x1, Pallas kernels, local(): pl.pallas_call(functools.partial(lora_kernel, lora_dims, rank), out_shape...  9.6 us
    pallas_call x1, Pallas kernels, local(): pl.pallas_call(functools.partial(project_kernel, (steps, requests, capaci...  7.55 us
    all_to_all x1, starting transfers between devices, local(): lax.all_to_all(outgoing, ('tensor', 'pool'), split_axis=0, concat_axis=0,...  7.38 us
    all_to_all x1, waiting for transfers between devices, local(): lax.all_to_all(outgoing, ('tensor', 'pool'), split_axis=0, concat_axis=0,...  6.88 us
    ppermute x6, starting transfers between devices, swapped(): return lax.ppermute(value, axis, pairs)  4.84 us
    pallas_call x1, Pallas kernels, local(): pl.pallas_call(functools.partial(stage_kernel, lora_dims), out_shape=[in_...  4.14 us
    pallas_call x2, Pallas kernels, local(): pl.pallas_call(functools.partial(send_kernel, attend_dims, half * (reques...  3.6 us
    pallas_call x2, Pallas kernels, local(): pl.pallas_call(functools.partial(own_kernel, attend_dims, half * (request...  3.58 us
  transfers between devices with their start and end apart: 7, of which 3 were waited for; matrix products, arithmetic and copies ran while one was open for 0% of the time, Pallas kernels for 27%

profile of v3, /device:TPU:0, one launch (start us, length us, event | category | flops | bytes accessed | tf_op | source)
XLA Modules:
  0.0 57.0 jit_solution(874528955653738701)
XLA Ops:
  0.0 4.1 %stage.1 = (bf16[128,8192]{1,0:T(8,128)(2,1)S(1)}, bf16[512,8192]{1,0:T(8,128)(2,1)S(1)}, s32[1,64]{1,0:T(1,128)S(1)}, s32[1,256]{1,0:T(1,128)S(1)}, bf16[16,819...) custom-call(bf16[128,8192]{1,0:T(8,128)(2,1)} %bitcast.16, ...), custom_call_target="tpu_custom_call" | custom-call | tf_op jit(solution)/shard_map/stage/pallas_call | solution.py:503
  4.1 0.5 collective-permute-start
  4.7 0.1 collective-permute-start.1
  4.7 2.2 %more.1.down_second = bf16[256,8192]{1,0:T(8,128)(2,1)S(1)} custom-call(bf16[1024,8192]{1,0:T(8,128)(2,1)} %bitcast.12, s32[16,1]{1,0:T(8,128)S(1)} %get-tuple-element.30.after.own_rows_ref), custom_call_target="tpu_custom_call" | custom-call | bytes 16777216 | tf_op jit(solution)/shard_map/more/pallas_call | solution.py:524
  7.0 0.0 collective-permute-done.1.other_rows_ref
  7.0 0.0 copy-start
  7.0 0.0 copy-start.1
  7.0 9.6 %lora.1 = bf16[16,16,1024]{2,1,0:T(8,128)(2,1)} custom-call(bf16[16,8192]{1,0:T(8,128)(2,1)S(1)} %get-tuple-element.29.own_ref, s32[16,1]{1,0:T(8,128)S(1)} %get-tuple-element.30.after.own_rows_ref, bf16[16,8192]{1,0:T(8,128)(2,1)S(1)} %collective-permute-done.other_ref, s32[16,1]{1,0:T(8,128)S(1)} %collective-permute-done.1.other_rows_ref, ...), custom_call_target="tpu_custom_call" | custom-call | flops 1073741824 | bytes 16777216 | tf_op jit(solution)/shard_map/lora/pallas_call | solution.py:535
  16.6 7.4 %all-to-all-start = ((bf16[16,16,1024]{2,1,0:T(8,128)(2,1)}), bf16[16,16,1024]{2,1,0:T(8,128)(2,1)S(1)}, u32[]{:S(2)}, u32[]{:S(2)}) async-start(bf16[16,16,1024]{2,1,0:T(8,128)(2,1)} %lora.1), calls=%async_computation | async-start | bytes 1048576 | tf_op jit(solution)/shard_map/all_to_all | solution.py:564
  24.0 7.5 %project.1 = (f32[128,1024]{1,0:T(8,128)S(1)}, bf16[128,128]{1,0:T(8,128)(2,1)S(1)}, f32[128,128]{1,0:T(8,128)S(1)}, f32[128,128]{1,0:T(8,128)S(1)}, bf16[128,256]{1,0:T(8,128)(2,1)S(1)}) custom-call(bf16[128,8192]{1,0:T(8,128)(2,1)S(1)} %get-tuple-element.37.states_ref, s32[1,64]{1,0:T(1,128)S(1)} %get-tuple-element.38.adapters_ref, ...), custom_call_target="tpu_custom_call" | custom-call | flops 2147483648 | bytes 16777216 | tf_op jit(solution)/shard_map/project/pallas_call | solution.py:572
  31.6 6.9 %all-to-all-done = bf16[16,16,1024]{2,1,0:T(8,128)(2,1)S(1)} async-done(((bf16[16,16,1024]{2,1,0:T(8,128)(2,1)}), bf16[16,16,1024]{2,1,0:T(8,128)(2,1)S(1)}, u32[]{:S(2)}, u32[]{:S(2)}) %all-to-all-start) | async-done | bytes 524320 | tf_op jit(solution)/shard_map/all_to_all | solution.py:564
  38.5 0.5 query.1
  38.9 0.5 collective-permute-start.2
  39.4 1.6 %collective-permute-start.3 = (bf16[512,128]{1,0:T(8,128)(2,1)S(1)}, bf16[512,128]{1,0:T(8,128)(2,1)S(1)}, u32[]{:S(2)}, u32[]{:S(2)}) collective-permute-start(bf16[512,128]{1,0:T(8,128)(2,1)S(1)} %get-tuple-element.50.query_ref), channel_id=1, source_target_pairs={{0,2},{2,0},{4,6},{6,4},{8,10},{10,8},{12,14},{14,12},{1,3},{3,1},... | collective-permute-start | bytes 393224 | tf_op jit(solution)/shard_map/ppermute | solution.py:22
  41.0 2.2 %load.1.cache_ref = bf16[64,2,128,128]{3,2,1,0:T(8,128)(2,1)S(1)} custom-call(bf16[64,2,128,128]{3,2,1,0:T(8,128)(2,1)} %bitcast.15, bf16[640,128]{1,0:T(8,128)(2,1)S(1)} %get-tuple-element.47.after.sent_ref.query_ref), custom_call_target="tpu_custom_call" | custom-call | bytes 8388608 | tf_op jit(solution)/shard_map/load/pallas_call | solution.py:623
  43.2 2.8 %collective-permute-done.2.got_ref.query_ref = bf16[640,128]{1,0:T(8,128)(2,1)S(1)} collective-permute-done((bf16[640,128]{1,0:T(8,128)(2,1)S(1)}, bf16[640,128]{1,0:T(8,128)(2,1)S(1)}, u32[]{:S(2)}, u32[]{:S(2)}) %collective-permute-start.2) | collective-permute-done | bytes 163872 | tf_op jit(solution)/shard_map/ppermute | solution.py:22
  46.1 1.8 %send.3 = bf16[528,128]{1,0:T(8,128)(2,1)S(1)} custom-call(s32[64]{0:T(128)S(1)} %copy-done, bf16[640,128]{1,0:T(8,128)(2,1)S(1)} %get-tuple-element.47.after.sent_ref.query_ref, bf16[640,128]{1,0:T(8,128)(2,1)S(1)} %collective-permute-done.2.got_ref.query_ref, bf16[640,128]{1,0:T(8,128)(2,1)S(1)} %collective-permute-done.2.got_ref.query_ref, ...), custom_call_target="tpu_custom_call" | custom-call | flops 33554432 | bytes 2097152 | tf_op jit(solution)/shard_map/send/pallas_call | solution.py:653
  47.9 0.5 collective-permute-start.4
  48.3 1.8 %send.2 = bf16[528,128]{1,0:T(8,128)(2,1)S(1)} custom-call(s32[64]{0:T(128)S(1)} %copy-done, bf16[640,128]{1,0:T(8,128)(2,1)S(1)} %get-tuple-element.47.after.sent_ref.query_ref, bf16[640,128]{1,0:T(8,128)(2,1)S(1)} %collective-permute-done.2.got_ref.query_ref, bf16[512,128]{1,0:T(8,128)(2,1)S(1)} %collective-permute-done.3.query_ref, ...), custom_call_target="tpu_custom_call" | custom-call | flops 33554432 | bytes 2097152 | tf_op jit(solution)/shard_map/send/pallas_call | solution.py:653
  50.1 1.7 %collective-permute-start.5 = (bf16[528,128]{1,0:T(8,128)(2,1)S(1)}, bf16[528,128]{1,0:T(8,128)(2,1)S(1)}, u32[]{:S(2)}, u32[]{:S(2)}) collective-permute-start(bf16[528,128]{1,0:T(8,128)(2,1)S(1)} %send.2), channel_id=1, source_target_pairs={{0,2},{2,0},{4,6},{6,4},{8,10},{10,8},{12,14},{14,12},{1,3},{3,1},... | collective-permute-start | bytes 405512 | tf_op jit(solution)/shard_map/ppermute | solution.py:22
  51.8 1.8 %own.2 = (f32[512,128]{1,0:T(8,128)S(1)}, f32[4,128]{1,0:T(4,128)S(1)}) custom-call(s32[64]{0:T(128)S(1)} %copy-done, bf16[640,128]{1,0:T(8,128)(2,1)S(1)} %get-tuple-element.47.after.sent_ref.query_ref, bf16[640,128]{1,0:T(8,128)(2,1)S(1)} %collective-permute-done.2.got_ref.query_ref, bf16[640,128]{1,0:T(8,128)(2,1)S(1)} %get-tuple-element.47.after.sent_ref.query_ref, ...), custom_call_target="tpu_custom_call" | custom-call | flops 33554432 | bytes 2097152 | tf_op jit(solution)/shard_map/own/pallas_call | solution.py:667
  53.6 1.8 %own.3 = (f32[512,128]{1,0:T(8,128)S(1)}, f32[4,128]{1,0:T(4,128)S(1)}) custom-call(s32[64]{0:T(128)S(1)} %copy-done, bf16[640,128]{1,0:T(8,128)(2,1)S(1)} %get-tuple-element.47.after.sent_ref.query_ref, bf16[640,128]{1,0:T(8,128)(2,1)S(1)} %collective-permute-done.2.got_ref.query_ref, bf16[512,128]{1,0:T(8,128)(2,1)S(1)} %get-tuple-element.50.query_ref, ...), custom_call_target="tpu_custom_call" | custom-call | flops 33554432 | bytes 2097152 | tf_op jit(solution)/shard_map/own/pallas_call | solution.py:667
  55.4 0.4 collective-permute-done.5.refs_5_
  55.8 1.2 %merge.1 = bf16[128,1024]{1,0:T(8,128)(2,1)} custom-call(f32[512,128]{1,0:T(8,128)S(1)} %get-tuple-element.48.refs_0_, f32[4,128]{1,0:T(4,128)S(1)} %get-tuple-element.49.refs_1_, bf16[528,128]{1,0:T(8,128)(2,1)S(1)} %collective-permute-done.4.refs_2_, f32[512,128]{1,0:T(8,128)S(1)} %get-tuple-element.51.refs_3_, f32[4,128]{1,0:T(4,128)S(1)} %get-tuple-element.52.refs_4_, ...), custom_call_target="tpu_custom_call" | custom-call | tf_op jit(solution)/shard_map/merge/pallas_call | solution.py:681
  (5 shorter events, 0.0 us)
Async XLA Ops:
  4.1 2.8 %collective-permute-start = (bf16[16,8192]{1,0:T(8,128)(2,1)S(1)}, bf16[16,8192]{1,0:T(8,128)(2,1)S(1)}, u32[]{:S(2)}, u32[]{:S(2)}) collective-permute-start(bf16[16,8192]{1,0:T(8,128)(2,1)S(1)} %get-tuple-element.31), channel_id=1, source_target_pairs={{0,1},{1,0},{2,3},{3,2},{4,5},{5,4},{6,7},{7,6},{8,9},{9,8},{10,11... | collective-permute-start | bytes 786440 | tf_op jit(solution)/shard_map/ppermute | solution.py:22
  4.7 2.3 %collective-permute-start.1 = (s32[16,1]{1,0:T(8,128)S(1)}, s32[16,1]{1,0:T(8,128)S(1)}, u32[]{:S(2)}, u32[]{:S(2)}) collective-permute-start(s32[16,1]{1,0:T(8,128)S(1)} %get-tuple-element.32), channel_id=1, source_target_pairs={{0,1},{1,0},{2,3},{3,2},{4,5},{5,4},{6,7},{7,6},{8,9},{9,8},{10,11... | collective-permute-start | bytes 200 | tf_op jit(solution)/shard_map/ppermute | solution.py:22
  7.0 17.0 %copy-start = (s32[64]{0:T(128)S(1)}, s32[64]{0:T(128)}, u32[]{:S(2)}) copy-start(s32[64]{0:T(128)} %lengths_ref.7) | copy-start | bytes 772
  7.0 17.0 %copy-start.1 = (f32[1,128]{1,0:T(1,128)S(1)}, f32[1,128]{1,0:T(1,128)}, u32[]{:S(2)}) copy-start(f32[1,128]{1,0:T(1,128)} %constant.2.clone.freq_ref) | copy-start | bytes 1540
  16.6 21.9 %all-to-all-start = ((bf16[16,16,1024]{2,1,0:T(8,128)(2,1)}), bf16[16,16,1024]{2,1,0:T(8,128)(2,1)S(1)}, u32[]{:S(2)}, u32[]{:S(2)}) async-start(bf16[16,16,1024]{2,1,0:T(8,128)(2,1)} %lora.1), calls=%async_computation | async-start | bytes 1048576 | tf_op jit(solution)/shard_map/all_to_all | solution.py:564
  38.9 7.1 %collective-permute-start.2 = (bf16[640,128]{1,0:T(8,128)(2,1)S(1)}, bf16[640,128]{1,0:T(8,128)(2,1)S(1)}, u32[]{:S(2)}, u32[]{:S(2)}) collective-permute-start(bf16[640,128]{1,0:T(8,128)(2,1)S(1)} %get-tuple-element.47.after.sent_ref.query_ref), channel_id=1, source_target_pairs={{0,2},{2,0},{4,6},{6,4},{8,10},{10,8},{12,14},{14,12},{1,3},{3,1},... | collective-permute-start | bytes 491528 | tf_op jit(solution)/shard_map/ppermute | solution.py:22
  39.4 8.9 %collective-permute-start.3 = (bf16[512,128]{1,0:T(8,128)(2,1)S(1)}, bf16[512,128]{1,0:T(8,128)(2,1)S(1)}, u32[]{:S(2)}, u32[]{:S(2)}) collective-permute-start(bf16[512,128]{1,0:T(8,128)(2,1)S(1)} %get-tuple-element.50.query_ref), channel_id=1, source_target_pairs={{0,2},{2,0},{4,6},{6,4},{8,10},{10,8},{12,14},{14,12},{1,3},{3,1},... | collective-permute-start | bytes 393224 | tf_op jit(solution)/shard_map/ppermute | solution.py:22
  47.9 7.6 %collective-permute-start.4 = (bf16[528,128]{1,0:T(8,128)(2,1)S(1)}, bf16[528,128]{1,0:T(8,128)(2,1)S(1)}, u32[]{:S(2)}, u32[]{:S(2)}) collective-permute-start(bf16[528,128]{1,0:T(8,128)(2,1)S(1)} %send.3), channel_id=1, source_target_pairs={{0,2},{2,0},{4,6},{6,4},{8,10},{10,8},{12,14},{14,12},{1,3},{3,1},... | collective-permute-start | bytes 405512 | tf_op jit(solution)/shard_map/ppermute | solution.py:22
  50.1 5.7 %collective-permute-start.5 = (bf16[528,128]{1,0:T(8,128)(2,1)S(1)}, bf16[528,128]{1,0:T(8,128)(2,1)S(1)}, u32[]{:S(2)}, u32[]{:S(2)}) collective-permute-start(bf16[528,128]{1,0:T(8,128)(2,1)S(1)} %send.2), channel_id=1, source_target_pairs={{0,2},{2,0},{4,6},{6,4},{8,10},{10,8},{12,14},{14,12},{1,3},{3,1},... | collective-permute-start | bytes 405512 | tf_op jit(solution)/shard_map/ppermute | solution.py:22

commit v4 on v3

--- a/solution.py
+++ b/solution.py
@@ -276,7 +276,7 @@
 
 
 def query_kernel(
-    dims, terms_ref, spread_ref, projected_ref, piece_ref, cosine_ref, sine_ref, first_ref, second_ref, packed
+    dims, terms_ref, spread_ref, projected_ref, cosine_ref, sine_ref, first_ref, second_ref, packed
 ):
     steps, requests, heads, head_width = dims
     correction = jnp.dot(spread_ref[...], terms_ref[...], preferred_element_type=F32)
@@ -292,8 +292,7 @@
                 step * requests : (step + 1) * requests
             ]
     half = count // 2
-    first_ref[:half, :] = packed[:half, :].astype(BF)
-    first_ref[half:, :] = piece_ref[...]
+    first_ref[...] = packed[:half, :].astype(BF)
     second_ref[...] = packed[half:, :].astype(BF)
 
 
@@ -381,8 +380,7 @@
 def own_kernel(
     dims, first, lengths_ref, sent_ref, got_ref, query_ref, cache_ref, out_ref, level_ref, *scratch
 ):
-    count = out_ref.shape[0]
-    keys, vals = new_pieces(sent_ref[count:, :], got_ref[count:, :])
+    keys, vals = new_pieces(sent_ref[...], got_ref[...])
 
     def store(at, rows, result, level):
         out_ref[pl.ds(at * rows, rows), :] = result
@@ -399,7 +397,7 @@
 ):
     lines = levels.shape[0]
     count = lines * 128
-    keys, vals = new_pieces(sent_ref[count:, :], got_ref[count:, :])
+    keys, vals = new_pieces(sent_ref[...], got_ref[...])
 
     def store(at, rows, result, level):
         out_ref[pl.ds(at * rows, rows), :] = result.astype(BF)
@@ -602,21 +600,23 @@
         in_hbm(key_value_weight),
     )
 
+    other_piece = swapped(own_piece, "tensor", 0)
+    spread, other_piece = lax.optimization_barrier((spread, other_piece))
     dims = (steps, requests, heads, head_width)
     packed_rows = count * heads
     half_rows = packed_rows // 2
     sent, sent_second = pl.pallas_call(
         functools.partial(query_kernel, dims),
         out_shape=[
-            jax.ShapeDtypeStruct((half_rows + count, head_width), BF),
+            jax.ShapeDtypeStruct((half_rows, head_width), BF),
             jax.ShapeDtypeStruct((half_rows, head_width), BF),
         ],
-        in_specs=whole(*range(6)),
+        in_specs=whole(*range(5)),
         out_specs=whole(*range(2)),
         scratch_shapes=[pltpu.VMEM((packed_rows, head_width), F32)],
         compiler_params=vmem_limit(8),
         name="query",
-    )(terms, spread, projected, own_piece, cosine, sine)
+    )(terms, spread, projected, cosine, sine)
     got = swapped(sent, "tensor", 0)
     got_second = swapped(sent_second, "tensor", 0)
 
@@ -659,7 +659,7 @@
             compiler_params=vmem_limit(16),
             cost_estimate=cost,
             name="send",
-        )(lengths, sent, got, other_query, cache_here)
+        )(lengths, own_piece, other_piece, other_query, cache_here)
         partials.append(swapped(sending, "tensor", 0))
     queries = lax.optimization_barrier((sent, sent_second, sending))
     merging = []
@@ -676,7 +676,7 @@
             compiler_params=vmem_limit(16),
             cost_estimate=cost,
             name="own",
-        )(lengths, sent, got, queries[half], cache_here)
+        )(lengths, own_piece, other_piece, queries[half], cache_here)
         merging += [own, level, partials[half]]
     attended = pl.pallas_call(
         functools.partial(merge_kernel, dims),

time: 57.2 us -> 56.5 us (0.988)
  waiting for transfers between devices: 10.1 us -> 7.44 us
  starting transfers between devices: 12.2 us -> 14.2 us
    all_to_all x1, waiting for transfers between devices: 6.88 us -> 2.9 us  [local(): lax.all_to_all(outgoing, ('tensor', 'pool'), split_axis=0, concat_axis=0,...]
    ppermute x6 -> x7, starting transfers between devices: 4.84 us -> 6.82 us  [swapped(): return lax.ppermute(value, axis, pairs)]
    ppermute x6 -> x7, waiting for transfers between devices: 3.24 us -> 4.54 us  [swapped(): return lax.ppermute(value, axis, pairs)]
  transfers between devices with their start and end apart: 7 -> 8, of which waited for: 3 -> 4; matrix products, arithmetic and copies ran while one was open for 0% -> 0% of each run, Pallas kernels for 27% -> 28%
where the time goes in v4:
time: 56.5 us; the launch traced here: 56.3 us
  Pallas kernels  34.5 us (61%)
  starting transfers between devices  14.2 us (25%)
  waiting for transfers between devices  7.44 us (13%)
    pallas_call x1, Pallas kernels, local(): pl.pallas_call(functools.partial(lora_kernel, lora_dims, rank), out_shape...  9.6 us
    pallas_call x1, Pallas kernels, local(): pl.pallas_call(functools.partial(project_kernel, (steps, requests, capaci...  7.55 us
    all_to_all x1, starting transfers between devices, local(): lax.all_to_all(outgoing, ('tensor', 'pool'), split_axis=0, concat_axis=0,...  7.38 us
    ppermute x7, starting transfers between devices, swapped(): return lax.ppermute(value, axis, pairs)  6.82 us
    ppermute x7, waiting for transfers between devices, swapped(): return lax.ppermute(value, axis, pairs)  4.54 us
    pallas_call x1, Pallas kernels, local(): pl.pallas_call(functools.partial(stage_kernel, lora_dims), out_shape=[in_...  4.14 us
    pallas_call x2, Pallas kernels, local(): pl.pallas_call(functools.partial(send_kernel, attend_dims, half * (reques...  3.6 us
    pallas_call x2, Pallas kernels, local(): pl.pallas_call(functools.partial(own_kernel, attend_dims, half * (request...  3.58 us
  transfers between devices with their start and end apart: 8, of which 4 were waited for; matrix products, arithmetic and copies ran while one was open for 0% of the time, Pallas kernels for 28%

profile of v4, /device:TPU:0, one launch (start us, length us, event | category | flops | bytes accessed | tf_op | source)
XLA Modules:
  0.0 56.3 jit_solution(4292973490170420191)
XLA Ops:
  0.0 4.1 %stage.1 = (bf16[128,8192]{1,0:T(8,128)(2,1)S(1)}, bf16[512,8192]{1,0:T(8,128)(2,1)S(1)}, s32[1,64]{1,0:T(1,128)S(1)}, s32[1,256]{1,0:T(1,128)S(1)}, bf16[16,819...) custom-call(bf16[128,8192]{1,0:T(8,128)(2,1)} %bitcast.16, ...), custom_call_target="tpu_custom_call" | custom-call | tf_op jit(solution)/shard_map/stage/pallas_call | solution.py:501
  4.1 0.5 collective-permute-start
  4.7 0.1 collective-permute-start.1
  4.7 2.2 %more.1.down_second = bf16[256,8192]{1,0:T(8,128)(2,1)S(1)} custom-call(bf16[1024,8192]{1,0:T(8,128)(2,1)} %bitcast.12, s32[16,1]{1,0:T(8,128)S(1)} %get-tuple-element.35.after.own_rows_ref), custom_call_target="tpu_custom_call" | custom-call | bytes 16777216 | tf_op jit(solution)/shard_map/more/pallas_call | solution.py:522
  7.0 0.0 copy-start.1
  7.0 9.6 %lora.1 = bf16[16,16,1024]{2,1,0:T(8,128)(2,1)} custom-call(bf16[16,8192]{1,0:T(8,128)(2,1)S(1)} %get-tuple-element.34.own_ref, s32[16,1]{1,0:T(8,128)S(1)} %get-tuple-element.35.after.own_rows_ref, bf16[16,8192]{1,0:T(8,128)(2,1)S(1)} %collective-permute-done.other_ref, s32[16,1]{1,0:T(8,128)S(1)} %collective-permute-done.1.other_rows_ref, ...), custom_call_target="tpu_custom_call" | custom-call | flops 1073741824 | bytes 16777216 | tf_op jit(solution)/shard_map/lora/pallas_call | solution.py:533
  16.6 7.4 %all-to-all-start = ((bf16[16,16,1024]{2,1,0:T(8,128)(2,1)}), bf16[16,16,1024]{2,1,0:T(8,128)(2,1)S(1)}, u32[]{:S(2)}, u32[]{:S(2)}) async-start(bf16[16,16,1024]{2,1,0:T(8,128)(2,1)} %lora.1), calls=%async_computation | async-start | bytes 1048576 | tf_op jit(solution)/shard_map/all_to_all | solution.py:562
  24.0 7.6 %project.1 = (f32[128,1024]{1,0:T(8,128)S(1)}, bf16[128,128]{1,0:T(8,128)(2,1)S(1)}, f32[128,128]{1,0:T(8,128)S(1)}, f32[128,128]{1,0:T(8,128)S(1)}, bf16[128,256]{1,0:T(8,128)(2,1)S(1)}) custom-call(bf16[128,8192]{1,0:T(8,128)(2,1)S(1)} %get-tuple-element.39.states_ref, s32[1,64]{1,0:T(1,128)S(1)} %get-tuple-element.40.adapters_ref, ...), custom_call_target="tpu_custom_call" | custom-call | flops 2147483648 | bytes 16777216 | tf_op jit(solution)/shard_map/project/pallas_call | solution.py:570
  31.6 2.0 %collective-permute-start.2 = (bf16[128,128]{1,0:T(8,128)(2,1)S(1)}, bf16[128,128]{1,0:T(8,128)(2,1)S(1)}, u32[]{:S(2)}, u32[]{:S(2)}) collective-permute-start(bf16[128,128]{1,0:T(8,128)(2,1)S(1)} %get-tuple-element.42.sent_ref), channel_id=1, source_target_pairs={{0,2},{2,0},{4,6},{6,4},{8,10},{10,8},{12,14},{14,12},{1,3},{3,1},... | collective-permute-start | bytes 98312 | tf_op jit(solution)/shard_map/ppermute | solution.py:22
  33.6 2.0 %collective-permute-done.2.got_ref = bf16[128,128]{1,0:T(8,128)(2,1)S(1)} collective-permute-done((bf16[128,128]{1,0:T(8,128)(2,1)S(1)}, bf16[128,128]{1,0:T(8,128)(2,1)S(1)}, u32[]{:S(2)}, u32[]{:S(2)}) %collective-permute-start.2) | collective-permute-done | bytes 32800 | tf_op jit(solution)/shard_map/ppermute | solution.py:22
  35.6 2.9 %all-to-all-done = bf16[16,16,1024]{2,1,0:T(8,128)(2,1)S(1)} async-done(((bf16[16,16,1024]{2,1,0:T(8,128)(2,1)}), bf16[16,16,1024]{2,1,0:T(8,128)(2,1)S(1)}, u32[]{:S(2)}, u32[]{:S(2)}) %all-to-all-start) | async-done | bytes 524320 | tf_op jit(solution)/shard_map/all_to_all | solution.py:562
  38.5 0.5 query.1
  38.9 0.5 collective-permute-start.4
  39.4 1.6 %collective-permute-start.3 = (bf16[512,128]{1,0:T(8,128)(2,1)S(1)}, bf16[512,128]{1,0:T(8,128)(2,1)S(1)}, u32[]{:S(2)}, u32[]{:S(2)}) collective-permute-start(bf16[512,128]{1,0:T(8,128)(2,1)S(1)} %get-tuple-element.54.query_ref), channel_id=1, source_target_pairs={{0,2},{2,0},{4,6},{6,4},{8,10},{10,8},{12,14},{14,12},{1,3},{3,1},... | collective-permute-start | bytes 393224 | tf_op jit(solution)/shard_map/ppermute | solution.py:22
  41.0 2.2 %load.1.cache_ref = bf16[64,2,128,128]{3,2,1,0:T(8,128)(2,1)S(1)} custom-call(bf16[64,2,128,128]{3,2,1,0:T(8,128)(2,1)} %bitcast.15, bf16[512,128]{1,0:T(8,128)(2,1)S(1)} %get-tuple-element.51.after.query_ref), custom_call_target="tpu_custom_call" | custom-call | bytes 8388608 | tf_op jit(solution)/shard_map/load/pallas_call | solution.py:623
  43.2 2.1 %collective-permute-done.4.query_ref = bf16[512,128]{1,0:T(8,128)(2,1)S(1)} collective-permute-done((bf16[512,128]{1,0:T(8,128)(2,1)S(1)}, bf16[512,128]{1,0:T(8,128)(2,1)S(1)}, u32[]{:S(2)}, u32[]{:S(2)}) %collective-permute-start.4) | collective-permute-done | bytes 131104 | tf_op jit(solution)/shard_map/ppermute | solution.py:22
  45.3 1.8 %send.3 = bf16[528,128]{1,0:T(8,128)(2,1)S(1)} custom-call(s32[64]{0:T(128)S(1)} %copy-done, bf16[128,128]{1,0:T(8,128)(2,1)S(1)} %get-tuple-element.42.sent_ref, bf16[128,128]{1,0:T(8,128)(2,1)S(1)} %collective-permute-done.2.got_ref, bf16[512,128]{1,0:T(8,128)(2,1)S(1)} %collective-permute-done.4.query_ref, bf16[64,2,128,128]{3,2,1,0:T(8,128)(2,1)S(1)} %load.1.cache_ref), custom_call_target="tpu_custom_call" | custom-call | flops 33554432 | bytes 2097152 | tf_op jit(solution)/shard_map/send/pallas_call | solution.py:653
  47.2 0.5 collective-permute-start.5
  47.6 1.8 %send.2 = bf16[528,128]{1,0:T(8,128)(2,1)S(1)} custom-call(s32[64]{0:T(128)S(1)} %copy-done, bf16[128,128]{1,0:T(8,128)(2,1)S(1)} %get-tuple-element.42.sent_ref, bf16[128,128]{1,0:T(8,128)(2,1)S(1)} %collective-permute-done.2.got_ref, bf16[512,128]{1,0:T(8,128)(2,1)S(1)} %collective-permute-done.3.query_ref, bf16[64,2,128,128]{3,2,1,0:T(8,128)(2,1)S(1)} %load.1.cache_ref), custom_call_target="tpu_custom_call" | custom-call | flops 33554432 | bytes 2097152 | tf_op jit(solution)/shard_map/send/pallas_call | solution.py:653
  49.4 1.7 %collective-permute-start.6 = (bf16[528,128]{1,0:T(8,128)(2,1)S(1)}, bf16[528,128]{1,0:T(8,128)(2,1)S(1)}, u32[]{:S(2)}, u32[]{:S(2)}) collective-permute-start(bf16[528,128]{1,0:T(8,128)(2,1)S(1)} %send.2), channel_id=1, source_target_pairs={{0,2},{2,0},{4,6},{6,4},{8,10},{10,8},{12,14},{14,12},{1,3},{3,1},... | collective-permute-start | bytes 405512 | tf_op jit(solution)/shard_map/ppermute | solution.py:22
  51.1 1.8 %own.2 = (f32[512,128]{1,0:T(8,128)S(1)}, f32[4,128]{1,0:T(4,128)S(1)}) custom-call(s32[64]{0:T(128)S(1)} %copy-done, bf16[128,128]{1,0:T(8,128)(2,1)S(1)} %get-tuple-element.42.sent_ref, bf16[128,128]{1,0:T(8,128)(2,1)S(1)} %collective-permute-done.2.got_ref, bf16[512,128]{1,0:T(8,128)(2,1)S(1)} %get-tuple-element.51.after.query_ref, ...), custom_call_target="tpu_custom_call" | custom-call | flops 33554432 | bytes 2097152 | tf_op jit(solution)/shard_map/own/pallas_call | solution.py:667
  52.9 1.8 %own.3 = (f32[512,128]{1,0:T(8,128)S(1)}, f32[4,128]{1,0:T(4,128)S(1)}) custom-call(s32[64]{0:T(128)S(1)} %copy-done, bf16[128,128]{1,0:T(8,128)(2,1)S(1)} %get-tuple-element.42.sent_ref, bf16[128,128]{1,0:T(8,128)(2,1)S(1)} %collective-permute-done.2.got_ref, bf16[512,128]{1,0:T(8,128)(2,1)S(1)} %get-tuple-element.54.query_ref, ...), custom_call_target="tpu_custom_call" | custom-call | flops 33554432 | bytes 2097152 | tf_op jit(solution)/shard_map/own/pallas_call | solution.py:667
  54.7 0.4 collective-permute-done.6.refs_5_
  55.1 1.2 %merge.1 = bf16[128,1024]{1,0:T(8,128)(2,1)} custom-call(f32[512,128]{1,0:T(8,128)S(1)} %get-tuple-element.52.refs_0_, f32[4,128]{1,0:T(4,128)S(1)} %get-tuple-element.53.refs_1_, bf16[528,128]{1,0:T(8,128)(2,1)S(1)} %collective-permute-done.5.refs_2_, f32[512,128]{1,0:T(8,128)S(1)} %get-tuple-element.55.refs_3_, f32[4,128]{1,0:T(4,128)S(1)} %get-tuple-element.56.refs_4_, ...), custom_call_target="tpu_custom_call" | custom-call | tf_op jit(solution)/shard_map/merge/pallas_call | solution.py:681
  (7 shorter events, 0.0 us)
Async XLA Ops:
  4.1 2.8 %collective-permute-start = (bf16[16,8192]{1,0:T(8,128)(2,1)S(1)}, bf16[16,8192]{1,0:T(8,128)(2,1)S(1)}, u32[]{:S(2)}, u32[]{:S(2)}) collective-permute-start(bf16[16,8192]{1,0:T(8,128)(2,1)S(1)} %get-tuple-element.36), channel_id=1, source_target_pairs={{0,1},{1,0},{2,3},{3,2},{4,5},{5,4},{6,7},{7,6},{8,9},{9,8},{10,11... | collective-permute-start | bytes 786440 | tf_op jit(solution)/shard_map/ppermute | solution.py:22
  4.7 2.3 %collective-permute-start.1 = (s32[16,1]{1,0:T(8,128)S(1)}, s32[16,1]{1,0:T(8,128)S(1)}, u32[]{:S(2)}, u32[]{:S(2)}) collective-permute-start(s32[16,1]{1,0:T(8,128)S(1)} %get-tuple-element.37), channel_id=1, source_target_pairs={{0,1},{1,0},{2,3},{3,2},{4,5},{5,4},{6,7},{7,6},{8,9},{9,8},{10,11... | collective-permute-start | bytes 200 | tf_op jit(solution)/shard_map/ppermute | solution.py:22
  7.0 17.0 %copy-start = (s32[64]{0:T(128)S(1)}, s32[64]{0:T(128)}, u32[]{:S(2)}) copy-start(s32[64]{0:T(128)} %lengths_ref.7) | copy-start | bytes 772
  7.0 17.0 %copy-start.1 = (f32[1,128]{1,0:T(1,128)S(1)}, f32[1,128]{1,0:T(1,128)}, u32[]{:S(2)}) copy-start(f32[1,128]{1,0:T(1,128)} %constant.2.clone.freq_ref) | copy-start | bytes 1540
  16.6 21.9 %all-to-all-start = ((bf16[16,16,1024]{2,1,0:T(8,128)(2,1)}), bf16[16,16,1024]{2,1,0:T(8,128)(2,1)S(1)}, u32[]{:S(2)}, u32[]{:S(2)}) async-start(bf16[16,16,1024]{2,1,0:T(8,128)(2,1)} %lora.1), calls=%async_computation | async-start | bytes 1048576 | tf_op jit(solution)/shard_map/all_to_all | solution.py:562
  31.6 4.0 %collective-permute-start.2 = (bf16[128,128]{1,0:T(8,128)(2,1)S(1)}, bf16[128,128]{1,0:T(8,128)(2,1)S(1)}, u32[]{:S(2)}, u32[]{:S(2)}) collective-permute-start(bf16[128,128]{1,0:T(8,128)(2,1)S(1)} %get-tuple-element.42.sent_ref), channel_id=1, source_target_pairs={{0,2},{2,0},{4,6},{6,4},{8,10},{10,8},{12,14},{14,12},{1,3},{3,1},... | collective-permute-start | bytes 98312 | tf_op jit(solution)/shard_map/ppermute | solution.py:22
  38.9 6.4 %collective-permute-start.4 = (bf16[512,128]{1,0:T(8,128)(2,1)S(1)}, bf16[512,128]{1,0:T(8,128)(2,1)S(1)}, u32[]{:S(2)}, u32[]{:S(2)}) collective-permute-start(bf16[512,128]{1,0:T(8,128)(2,1)S(1)} %get-tuple-element.51.after.query_ref), channel_id=1, source_target_pairs={{0,2},{2,0},{4,6},{6,4},{8,10},{10,8},{12,14},{14,12},{1,3},{3,1},... | collective-permute-start | bytes 393224 | tf_op jit(solution)/shard_map/ppermute | solution.py:22
  39.4 8.2 %collective-permute-start.3 = (bf16[512,128]{1,0:T(8,128)(2,1)S(1)}, bf16[512,128]{1,0:T(8,128)(2,1)S(1)}, u32[]{:S(2)}, u32[]{:S(2)}) collective-permute-start(bf16[512,128]{1,0:T(8,128)(2,1)S(1)} %get-tuple-element.54.query_ref), channel_id=1, source_target_pairs={{0,2},{2,0},{4,6},{6,4},{8,10},{10,8},{12,14},{14,12},{1,3},{3,1},... | collective-permute-start | bytes 393224 | tf_op jit(solution)/shard_map/ppermute | solution.py:22
  47.2 7.6 %collective-permute-start.5 = (bf16[528,128]{1,0:T(8,128)(2,1)S(1)}, bf16[528,128]{1,0:T(8,128)(2,1)S(1)}, u32[]{:S(2)}, u32[]{:S(2)}) collective-permute-start(bf16[528,128]{1,0:T(8,128)(2,1)S(1)} %send.3), channel_id=1, source_target_pairs={{0,2},{2,0},{4,6},{6,4},{8,10},{10,8},{12,14},{14,12},{1,3},{3,1},... | collective-permute-start | bytes 405512 | tf_op jit(solution)/shard_map/ppermute | solution.py:22
  49.4 5.7 %collective-permute-start.6 = (bf16[528,128]{1,0:T(8,128)(2,1)S(1)}, bf16[528,128]{1,0:T(8,128)(2,1)S(1)}, u32[]{:S(2)}, u32[]{:S(2)}) collective-permute-start(bf16[528,128]{1,0:T(8,128)(2,1)S(1)} %send.2), channel_id=1, source_target_pairs={{0,2},{2,0},{4,6},{6,4},{8,10},{10,8},{12,14},{14,12},{1,3},{3,1},... | collective-permute-start | bytes 405512 | tf_op jit(solution)/shard_map/ppermute | solution.py:22
